TPU v7x, 128 devices: a whole 4x4x4 slice. The times are simulated.
128 devices in a mesh: pipe: 4 (over y), tensor: 8 (over x, core), dp: 4 (over z).
Axes of the slice: x: 4, y: 4, z: 4, core: 2. Of those that a mesh axis runs over, the one named last changes fastest.
Arguments:
- hidden: bfloat16 [16, 64, 16384], P('dp', None, ('pipe', 'tensor')), parts along dimension 0, may hold values from -200 to 200
- norm_gain: bfloat16 [16384], P(('pipe', 'tensor')), may hold values from 0.5 to 1.5
- head_weight: bfloat16 [16384, 24576], P(None, ('pipe', 'tensor')), may hold values from -0.5 to 0.5
Outputs:
- logits: bfloat16 [16, 64, 24576], P('dp', None, ('pipe', 'tensor')), parts along dimension 0
- probs: float32 [16, 64, 24576], P('dp', None, ('pipe', 'tensor')), parts along dimension 0
There are 4 independent parts, one for each index of `dp`. A program takes and returns all parts, laid end to end along the dimension named above; an argument that names none is the same for every part. Nothing has to cross between parts.
All inputs are finite; a program needn't handle non-finite values.
Results may differ from a plain program's by a relative error of at most 0.012.
Values may be sent and summed in bfloat16 or wider, within the bound.
No kernel may reach another device: no remote copies, remote signals or barrier semaphores. Data moves between devices by JAX's collectives and lax.ppermute only.
A program may use at most 128 MiB of HBM per device.

v0:
```python
import math

import jax
import jax.numpy as jnp
from jax import lax
from jax.sharding import PartitionSpec as P

min_p_log = math.log(0.1)
gate_sharpness = 4.0


def normalize(values, gain, total_sq, width):
    scale = lax.rsqrt(total_sq / width + 1e-05)
    return (values.astype(jnp.float32) * scale[..., None] * gain.astype(jnp.float32)).astype(
        jnp.bfloat16
    )


def score_rows(hidden, norm_gain, head_weight):
    count = hidden.shape[0] * hidden.shape[1]
    local_sq = jnp.sum(jnp.square(hidden.astype(jnp.float32)), axis=-1)
    total_sq = lax.psum(local_sq, ("pipe", "tensor"))
    width = hidden.shape[2] * lax.axis_size(("pipe", "tensor"))
    normed = normalize(hidden, norm_gain, total_sq, width)
    piece = lax.all_gather(normed, ("pipe", "tensor"), axis=2, tiled=True)
    flat_piece = piece.reshape(count, piece.shape[2])
    scores = jnp.dot(flat_piece, head_weight, preferred_element_type=jnp.float32)
    return scores.reshape(hidden.shape[0], hidden.shape[1], head_weight.shape[1])


def finish_rows(hidden, norm_gain, head_weight):
    scores = score_rows(hidden, norm_gain, head_weight)
    top = lax.pmax(jnp.max(scores, axis=-1), ("pipe", "tensor"))
    shifted = scores - top[..., None]
    kept = jnp.exp(shifted) * jax.nn.sigmoid(gate_sharpness * (shifted - min_p_log))
    mass = lax.psum(jnp.sum(kept, axis=-1), ("pipe", "tensor"))
    return (scores.astype(jnp.bfloat16), kept / mass[..., None])


def local(hidden, norm_gain, head_weight):
    return finish_rows(hidden, norm_gain, head_weight)


def solution(mesh):
    return jax.shard_map(
        local,
        mesh=mesh,
        in_specs=(
            P("dp", None, ("pipe", "tensor")),
            P(("pipe", "tensor")),
            P(None, ("pipe", "tensor")),
        ),
        out_specs=(P("dp", None, ("pipe", "tensor")), P("dp", None, ("pipe", "tensor"))),
        check_vma=False,
    )
```

profile of v0, /device:TPU:1, one launch (start us, length us, event | category | flops | bytes accessed | tf_op | source)
XLA Modules:
  0.0 286.9 jit_solution(5358605468508173957)
XLA Ops:
  7.2 0.0 all-gather.2.cloned.1.call-start
  7.2 0.7 convert_element_type.14
  7.9 1.1 fusion.2
  9.0 63.8 %psum.14 = f32[4,64]{1,0:T(4,128)S(1)} all-reduce(f32[4,64]{1,0:T(4,128)S(1)} %fusion.2), channel_id=1, replica_groups=mesh['pipe'=4,'tensor'=8,'dp'=4] {'pipe','tensor'}, use_global_device_ids=true, to_apply=%region_1.0 | all-reduce | flops 256 | bytes 2048 | tf_op jit(solution)/shard_map/psum | solution.py:22
  72.8 1.8 fusion.4
  74.6 0.0 all-gather.2.cloned.1.call-update
  74.6 61.6 %all-gather.2.cloned.1.call-done = bf16[4,64,16384]{2,1,0:T(8,128)(2,1)} async-done(((bf16[4,64,512]{2,1,0:T(8,128)(2,1)}), bf16[4,64,16384]{2,1,0:T(8,128)(2,1)}) %all-gather.2.cloned.1.call-update) | async-done | bytes 8388624 | tf_op jit(solution)/shard_map/all_gather | solution.py:25
  136.2 14.2 %fusion.6 = (f32[4,64]{1,0:T(4,128)S(1)}, f32[4,64,768]{2,1,0:T(8,128)S(1)}) fusion(bf16[4,64,16384]{2,1,0:T(8,128)(2,1)} %all-gather.2.cloned.1.call-done, bf16[16384,768]{1,0:T(8,128)(2,1)} %param.5), kind=kOutput, calls=%fused_computation.11 | convolution fusion | flops 6442647552 | bytes 34341888 | tf_op jit(solution)/shard_map/dot_general | solution.py:27
  150.4 62.3 %pmax.7 = f32[4,64]{1,0:T(4,128)S(1)} all-reduce(f32[4,64]{1,0:T(4,128)S(1)} %get-tuple-element.4), channel_id=1, replica_groups=mesh['pipe'=4,'tensor'=8,'dp'=4] {'pipe','tensor'}, use_global_device_ids=true, to_apply=%region_3.0 | all-reduce | flops 256 | bytes 2048 | tf_op jit(solution)/shard_map/pmax | solution.py:33
  212.6 0.5 fusion.5
  213.1 65.5 %psum.15 = f32[4,64]{1,0:T(4,128)S(1)} all-reduce(f32[4,64]{1,0:T(4,128)S(1)} %fusion.5), channel_id=1, replica_groups=mesh['pipe'=4,'tensor'=8,'dp'=4] {'pipe','tensor'}, use_global_device_ids=true, to_apply=%region_5.0 | all-reduce | flops 256 | bytes 2048 | tf_op jit(solution)/shard_map/psum | solution.py:36
  278.6 1.5 broadcast_divide_fusion
  (1 shorter events, 0.0 us)
Async XLA Ops:
  7.2 129.0 %all-gather.2.cloned.1.call-start = ((), (), s32[]{:S(2)}) async-start(), calls=%async_computation | async-start | bytes 8650752 | tf_op jit(solution)/shard_map/all_gather | solution.py:25
Sparse Core Ops, SparseCore 0:
  74.7 61.4 all-gather.1
where the time goes:
time: 287 us
  blocking collectives  192 us (67%)
  waiting for transfers between devices  61.6 us (21%)
  matrix products  14.2 us (5%)
  between operations  14 us (5%)
  other arithmetic  5.5 us (2%)
    psum x1, blocking collectives, finish_rows(): mass = lax.psum(jnp.sum(kept, axis=-1), ('pipe', 'tensor'))  65.5 us
    psum x1, blocking collectives, score_rows(): total_sq = lax.psum(local_sq, ('pipe', 'tensor'))  63.8 us
    pmax x1, blocking collectives, finish_rows(): top = lax.pmax(jnp.max(scores, axis=-1), ('pipe', 'tensor'))  62.3 us
    all_gather x1, waiting for transfers between devices, score_rows(): piece = lax.all_gather(normed, ('pipe', 'tensor'), axis=2, tiled=True)  61.6 us
    dot_general x1, matrix products, score_rows(): jnp.dot(flat_piece, head_weight, preferred_element_type=jnp.float32)  14.2 us
  transfers between devices with their start and end apart: 1, of which 1 were waited for; matrix products, arithmetic and copies ran while one was open for 0% of the time, Pallas kernels for 0%

commit v1 on v0

v1 whole, which is shorter than its diff:
```python
import math

import jax
import jax.numpy as jnp
from jax import lax
from jax.experimental import pallas as pl
from jax.experimental.pallas import tpu as pltpu
from jax.sharding import PartitionSpec as P

AXES = ("pipe", "tensor")
PEERS = 32
LANES = 128
min_p_log = math.log(0.1)
gate_sharpness = 4.0
VMEM_LIMIT = 48 * 1024 * 1024


def exchange(values):
    return lax.all_to_all(values, AXES, 0, 0, tiled=True)


def spread_rows(column, out_ref):
    rows = column.shape[0]
    across = jnp.broadcast_to(column, (rows, LANES)).T
    for part in range(rows // LANES):
        out_ref[:, part, :] = across[: out_ref.shape[0], part * LANES : (part + 1) * LANES]


def rows_of(parts):
    across = jnp.concatenate(parts, axis=1)
    return jnp.broadcast_to(across, (LANES, across.shape[1])).T


def head_kernel(scale_ref, gain_ref, piece_ref, weight_ref, scores_ref, logits_ref, top_ref):
    step = pl.program_id(0)
    scale = scale_ref[...]
    normed = [
        (piece_ref[core].astype(jnp.float32) * scale * gain_ref[core].astype(jnp.float32)).astype(
            jnp.bfloat16
        )
        for core in range(2)
    ]
    term = jnp.dot(
        jnp.concatenate(normed, axis=1), weight_ref[...], preferred_element_type=jnp.float32
    )

    @pl.when(step == 0)
    def _():
        scores_ref[...] = term

    @pl.when(step > 0)
    def _():
        scores_ref[...] += term

    @pl.when(step == pl.num_programs(0) - 1)
    def _():
        scores = scores_ref[...]
        logits_ref[...] = scores.astype(jnp.bfloat16)
        spread_rows(jnp.max(scores, axis=1, keepdims=True), top_ref)


def head(pieces, scale, gain, weight):
    peers, rows, width = pieces.shape
    columns = weight.shape[1]
    return pl.pallas_call(
        head_kernel,
        grid=(peers // 2,),
        in_specs=[
            pl.BlockSpec((rows, 1), lambda i: (0, 0)),
            pl.BlockSpec((2, 1, width), lambda i: (i, 0, 0)),
            pl.BlockSpec((2, rows, width), lambda i: (i, 0, 0)),
            pl.BlockSpec((2 * width, columns), lambda i: (i, 0)),
        ],
        out_specs=[
            pl.BlockSpec((rows, columns), lambda i: (0, 0)),
            pl.BlockSpec((rows, columns), lambda i: (0, 0)),
            pl.BlockSpec((PEERS, 2, LANES), lambda i: (0, 0, 0)),
        ],
        out_shape=[
            jax.ShapeDtypeStruct((rows, columns), jnp.float32),
            jax.ShapeDtypeStruct((rows, columns), jnp.bfloat16),
            jax.ShapeDtypeStruct((PEERS, 2, LANES), jnp.float32),
        ],
        compiler_params=pltpu.CompilerParams(vmem_limit_bytes=VMEM_LIMIT),
        name="head",
    )(scale, gain, pieces, weight)


def gate_kernel(tops_ref, scores_ref, kept_ref, mass_ref):
    top = rows_of([jnp.max(tops_ref[:, part, :], axis=0, keepdims=True) for part in range(2)])
    shifted = scores_ref[...] - top[:, :1]
    kept = jnp.exp(shifted) * jax.nn.sigmoid(gate_sharpness * (shifted - min_p_log))
    kept_ref[...] = kept
    spread_rows(jnp.sum(kept, axis=1, keepdims=True), mass_ref)


def gate(tops, scores):
    return pl.pallas_call(
        gate_kernel,
        out_shape=[
            jax.ShapeDtypeStruct(scores.shape, jnp.float32),
            jax.ShapeDtypeStruct(tops.shape, jnp.float32),
        ],
        compiler_params=pltpu.CompilerParams(vmem_limit_bytes=VMEM_LIMIT),
        name="gate",
    )(tops, scores)


def share_kernel(masses_ref, kept_ref, probs_ref):
    mass = rows_of([jnp.sum(masses_ref[:, part, :], axis=0, keepdims=True) for part in range(2)])
    probs_ref[...] = kept_ref[...] / mass[:, :1]


def share(masses, kept):
    return pl.pallas_call(
        share_kernel,
        out_shape=jax.ShapeDtypeStruct(kept.shape, jnp.float32),
        compiler_params=pltpu.CompilerParams(vmem_limit_bytes=VMEM_LIMIT),
        name="share",
    )(masses, kept)


def local(hidden, norm_gain, head_weight):
    micro, rows, width = hidden.shape
    flat = hidden.reshape(micro * rows, width)
    pieces = lax.all_gather(flat, AXES, axis=0)

    local_sq = jnp.sum(jnp.square(flat.astype(jnp.float32)), axis=-1)
    note = jnp.concatenate([local_sq, norm_gain.astype(jnp.float32)]).reshape(-1, LANES)
    notes = exchange(jnp.broadcast_to(note[None], (PEERS,) + note.shape)).reshape(PEERS, -1)
    total_sq = jnp.sum(notes[:, : micro * rows], axis=0)
    scale = lax.rsqrt(total_sq / (width * PEERS) + 1e-05)[:, None]
    gain = notes[:, None, micro * rows :]

    scores, logits, tops = head(pieces, scale, gain, head_weight)
    kept, masses = gate(exchange(tops), scores)
    probs = share(exchange(masses), kept)
    shape = (micro, rows, head_weight.shape[1])
    return logits.reshape(shape), probs.reshape(shape)


def solution(mesh):
    return jax.shard_map(
        local,
        mesh=mesh,
        in_specs=(
            P("dp", None, AXES),
            P(AXES),
            P(None, AXES),
        ),
        out_specs=(P("dp", None, AXES), P("dp", None, AXES)),
        check_vma=False,
    )
```

time: 287 us -> 120 us (0.42)
  blocking collectives: 192 us -> 39.3 us
  Pallas kernels: 0 us -> 22.4 us
  waiting for transfers between devices: 61.6 us -> 41.3 us
  matrix products: 14.2 us -> 0 us
  other arithmetic: 5.5 us -> 1.8 us
    psum x2 -> x0, blocking collectives: 129 us -> none  [the longest x1 65.5 us: finish_rows(): mass = lax.psum(jnp.sum(kept, axis=-1), ('pipe', 'tensor'))]
    pmax x1 -> x0, blocking collectives: 62.3 us -> none  [finish_rows(): top = lax.pmax(jnp.max(scores, axis=-1), ('pipe', 'tensor'))]
    all_to_all x0 -> x3, blocking collectives: none -> 39.3 us  [exchange(): return lax.all_to_all(values, AXES, 0, 0, tiled=True)]
    pallas_call x0 -> x3, Pallas kernels: none -> 22.4 us  [the longest x1 20.8 us: head(): pl.pallas_call(head_kernel, grid=(peers // 2,), in_specs=[pl.BlockSpec((r...]
    all_gather x1, waiting for transfers between devices: 61.6 us -> 40.6 us  [local(): pieces = lax.all_gather(flat, AXES, axis=0)]
    dot_general x1 -> x0, matrix products: 14.2 us -> none  [score_rows(): jnp.dot(flat_piece, head_weight, preferred_element_type=jnp.float32)]
  transfers between devices with their start and end apart: 1 -> 1, of which waited for: 1 -> 1; matrix products, arithmetic and copies ran while one was open for 0% -> 2% of each run, Pallas kernels for 0% -> 0%
where the time goes in v1:
time: 120 us; the launch traced here: 119 us
  waiting for transfers between devices  41.3 us (34%)
  blocking collectives  39.3 us (33%)
  Pallas kernels  22.4 us (19%)
  between operations  14.1 us (12%)
  other arithmetic  1.8 us (2%)
    all_gather x1, waiting for transfers between devices, local(): pieces = lax.all_gather(flat, AXES, axis=0)  40.6 us
    all_to_all x3, blocking collectives, exchange(): return lax.all_to_all(values, AXES, 0, 0, tiled=True)  39.3 us
    pallas_call x1, Pallas kernels, head(): pl.pallas_call(head_kernel, grid=(peers // 2,), in_specs=[pl.BlockSpec((r...  20.8 us
  transfers between devices with their start and end apart: 1, of which 1 were waited for; matrix products, arithmetic and copies ran while one was open for 2% of the time, Pallas kernels for 0%

profile of v1, /device:TPU:1, one launch (start us, length us, event | category | flops | bytes accessed | tf_op | source)
XLA Modules:
  0.0 119.2 jit_solution(12893444726866561587)
XLA Ops:
  7.2 0.0 all-gather.2.cloned.1.call-start
  7.2 0.7 all-gather.2.cloned.1.call-update
  7.9 0.7 convert_element_type.8
  8.6 1.1 multiply_reduce_fusion
  9.7 0.1 reduce_sum.21
  9.8 16.0 %all_to_all.15 = f32[32,6,128]{2,1,0:T(8,128)S(1)} all-to-all(f32[32,6,128]{2,1,0:T(8,128)S(1)} %broadcast_in_dim.12), channel_id=1, replica_groups=mesh['pipe'=4,'tensor'=8,'dp'=4] {'pipe','tensor'}, dimensions={0} | all-to-all | bytes 196608 | tf_op jit(solution)/shard_map/all_to_all | solution.py:19
  25.9 0.1 copy.6.scale_ref
  26.1 40.6 %all-gather.2.cloned.1.call-done.piece_ref = bf16[32,256,512]{2,1,0:T(8,128)(2,1)} async-done(((bf16[1,256,512]{2,1,0:T(8,128)(2,1)}), bf16[32,256,512]{2,1,0:T(8,128)(2,1)}) %all-gather.2.cloned.1.call-update) | async-done | bytes 8388624 | tf_op jit(solution)/shard_map/all_gather | solution.py:126
  66.7 20.8 %head.1 = (f32[256,768]{1,0:T(8,128)S(1)}, bf16[256,768]{1,0:T(8,128)(2,1)}, f32[32,2,128]{2,1,0:T(2,128)S(1)}) custom-call(f32[256,1]{1,0:T(8,128)S(1)} %copy.6.scale_ref, f32[32,1,512]{2,1,0:T(1,128)S(1)} %broadcast_in_dim.13.gain_ref, bf16[32,256,512]{2,1,0:T(8,128)(2,1)} %all-gather.2.cloned.1.call-done.piece_ref, bf16[16384,768]{1,0:T(8,128)(2,1)} %weight_ref.1), custom_call_target="tpu_custom_call" | custom-call | tf_op jit(solution)/shard_map/head/pallas_call | solution.py:65
  87.5 12.5 %all_to_all.16.tops_ref = f32[32,2,128]{2,1,0:T(2,128)S(1)} all-to-all(f32[32,2,128]{2,1,0:T(2,128)S(1)} %get-tuple-element.8), channel_id=1, replica_groups=mesh['pipe'=4,'tensor'=8,'dp'=4] {'pipe','tensor'}, dimensions={0} | all-to-all | bytes 65536 | tf_op jit(solution)/shard_map/all_to_all | solution.py:19
  100.0 0.5 gate.1
  100.5 10.7 %all_to_all.17.masses_ref = f32[32,2,128]{2,1,0:T(2,128)S(1)} all-to-all(f32[32,2,128]{2,1,0:T(2,128)S(1)} %get-tuple-element.10), channel_id=1, replica_groups=mesh['pipe'=4,'tensor'=8,'dp'=4] {'pipe','tensor'}, dimensions={0} | all-to-all | bytes 65536 | tf_op jit(solution)/shard_map/all_to_all | solution.py:19
  111.3 1.1 share.1
  (7 shorter events, 0.1 us)
Async XLA Ops:
  7.2 59.5 %all-gather.2.cloned.1.call-start = ((), (), s32[]{:S(2)}) async-start(), calls=%async_computation.3 | async-start | bytes 8650752 | tf_op jit(solution)/shard_map/all_gather | solution.py:126
Sparse Core Ops, SparseCore 0:
  10.3 56.3 all-gather.1

commit v2 on v1

v2 whole, which is shorter than its diff:
```python
import functools
import math

import jax
import jax.numpy as jnp
from jax import lax
from jax.experimental import pallas as pl
from jax.experimental.pallas import tpu as pltpu
from jax.sharding import PartitionSpec as P

AXES = ("pipe", "tensor")
RING = 4
CORES = 2
PEERS = RING * RING * CORES
LANES = 128
NOTE = 16
HALF = 128
GROUP = 4
AHEAD = 4
min_p_log = math.log(0.1)
gate_sharpness = 4.0
HEAD_VMEM = 54 * 1024 * 1024
SMALL_VMEM = 8 * 1024 * 1024

WHOLE = NOTE + 2 * HALF
TOP = NOTE + HALF
ROW_CUT, COLUMN_CUT = 208, 192
PLACES = {
    (0, 0): [("own", 0), ("own", NOTE, 2 * HALF)],
    (0, -1): [("left", 0), ("left", NOTE, 2 * HALF)],
    (0, 1): [("right", 0), ("right", NOTE, 2 * HALF)],
    (-1, 0): [("down", 0), ("down", NOTE, 2 * HALF)],
    (1, 0): [("up", 0), ("up", NOTE, 2 * HALF)],
    (0, 2): [("cross_a", 0), ("cross_a", NOTE, HALF), ("cross_b", 0, HALF)],
    (2, 0): [("over_a", 0), ("over_a", NOTE, HALF), ("over_b", 0, HALF)],
}
for _dy, _array in ((-1, "row_down"), (1, "row_up")):
    for _at, _dx in enumerate((-1, 1, 2)):
        PLACES[_dy, _dx] = [(_array, _at * TOP), (_array, _at * TOP + NOTE, HALF)]
PLACES[2, -1] = [("far_down", 0), ("far_down", NOTE, HALF)]
PLACES[2, 1] = [
    ("far_down", TOP),
    ("far_down", TOP + NOTE, ROW_CUT - TOP - NOTE),
    ("far_up", 0, 2 * TOP - ROW_CUT),
]
PLACES[2, 2] = [("far_up", 2 * TOP - ROW_CUT), ("far_up", 2 * TOP - ROW_CUT + NOTE, HALF)]
for _dx, _array in ((-1, "col_left"), (1, "col_right")):
    for _at, _dy in enumerate((-1, 1, 2)):
        PLACES[_dy, _dx].append((_array, _at * HALF, HALF))
PLACES[-1, 2].append(("far_left", 0, HALF))
PLACES[1, 2] += [
    ("far_left", HALF, COLUMN_CUT - HALF),
    ("far_right", 0, 2 * HALF - COLUMN_CUT),
]
PLACES[2, 2].append(("far_right", 2 * HALF - COLUMN_CUT, HALF))


def device(y, x, core):
    return (y % RING) * RING * CORES + (x % RING) * CORES + core


def fetch(value, dy, dx, core=0):
    pairs = [
        (device(y + dy, x + dx, c ^ core), device(y, x, c))
        for y in range(RING)
        for x in range(RING)
        for c in range(CORES)
    ]
    return lax.ppermute(value, AXES, pairs)


def exchange(values):
    return lax.all_to_all(values, AXES, 0, 0, tiled=True)


def spread_rows(column, out_ref):
    rows = column.shape[0]
    across = jnp.broadcast_to(column, (rows, LANES)).T
    for part in range(rows // LANES):
        out_ref[:, part, :] = across[: out_ref.shape[0], part * LANES : (part + 1) * LANES]


def rows_of(parts):
    across = jnp.concatenate(parts, axis=1)
    return jnp.broadcast_to(across, (LANES, across.shape[1])).T


def head_kernel(keys, *refs):
    block_refs = dict(zip(keys, refs))
    weight_ref, scores_ref, logits_ref, top_ref = refs[len(keys) : len(keys) + 4]
    raw_ref, note_ref, normed_ref, part_ref, raw_sems, note_sems, sems = refs[len(keys) + 4 :]
    pipe, tensor = lax.axis_index("pipe"), lax.axis_index("tensor")
    chip_x, core = tensor // CORES, lax.rem(tensor, CORES)
    _, rows, width = raw_ref.shape
    terms = [(chip, which) for chip in PLACES for which in range(CORES)]
    groups = len(terms) // GROUP

    def shard(term):
        chip, which = terms[term]
        (note_array, note_at), *runs = PLACES[chip]
        copies = [
            pltpu.make_async_copy(
                block_refs[which, note_array].at[pl.ds(note_at, NOTE), :],
                note_ref.at[term],
                note_sems.at[term],
            )
        ]
        at = 0
        for i, (array, start, count) in enumerate(runs):
            copies.append(
                pltpu.make_async_copy(
                    block_refs[which, array].at[pl.ds(start, count), :],
                    raw_ref.at[term, pl.ds(at, count), :],
                    raw_sems.at[term, i],
                )
            )
            at += count
        return copies

    def weights(group):
        copies = []
        for i, term in enumerate(range(group * GROUP, (group + 1) * GROUP)):
            (dy, dx), which = terms[term]
            chip_at = lax.rem(pipe + dy + RING, RING) * RING + lax.rem(chip_x + dx + RING, RING)
            peer = chip_at * CORES + (core if which == 0 else 1 - core)
            copies.append(
                pltpu.make_async_copy(
                    weight_ref.at[pl.ds(pl.multiple_of(peer * width, width), width), :],
                    part_ref.at[group % AHEAD, pl.ds(i * width, width), :],
                    sems.at[group % AHEAD, i],
                )
            )
        return copies

    def fetch_weights(group):
        for copy in weights(group):
            copy.start()

    for term in range(len(terms)):
        for copy in shard(term):
            copy.start()
    for group in range(AHEAD - 1):
        fetch_weights(group)
    squares = jnp.zeros((rows, LANES), jnp.float32)
    for term in range(len(terms)):
        for copy in shard(term):
            copy.wait()
        for lane in range(0, width, LANES):
            squares += jnp.square(raw_ref[term, :, lane : lane + LANES].astype(jnp.float32))
    total_sq = jnp.sum(squares, axis=1, keepdims=True)
    scale = lax.rsqrt(total_sq / (width * len(terms)) + 1e-05)

    def norm(group):
        for i, term in enumerate(range(group * GROUP, (group + 1) * GROUP)):
            gain = note_ref[term].astype(jnp.float32)[:1]
            normed_ref[group % 2, :, i * width : (i + 1) * width] = (
                raw_ref[term].astype(jnp.float32) * scale * gain
            ).astype(jnp.bfloat16)

    norm(0)
    for group in range(groups):
        for copy in weights(group):
            copy.wait()
        if group + AHEAD - 1 < groups:
            fetch_weights(group + AHEAD - 1)
        term = jnp.dot(
            normed_ref[group % 2], part_ref[group % AHEAD], preferred_element_type=jnp.float32
        )
        if group + 1 < groups:
            norm(group + 1)
        if group == 0:
            scores_ref[...] = term
        elif group < groups - 1:
            scores_ref[...] += term
        else:
            scores = scores_ref[...] + term
            scores_ref[...] = scores
            logits_ref[...] = scores.astype(jnp.bfloat16)
            spread_rows(jnp.max(scores, axis=1, keepdims=True), top_ref)


def head(blocks, weight):
    names = dict.fromkeys(place[0] for places in PLACES.values() for place in places)
    keys = [(which, array) for which in range(CORES) for array in names]
    rows, columns = 2 * HALF, weight.shape[1]
    width = weight.shape[0] // PEERS
    in_vmem = pl.BlockSpec(memory_space=pltpu.VMEM)
    return pl.pallas_call(
        functools.partial(head_kernel, keys),
        in_specs=[pl.BlockSpec(memory_space=pl.ANY)] * (len(keys) + 1),
        out_specs=[in_vmem] * 3,
        out_shape=[
            jax.ShapeDtypeStruct((rows, columns), jnp.float32),
            jax.ShapeDtypeStruct((rows, columns), jnp.bfloat16),
            jax.ShapeDtypeStruct((PEERS, rows // LANES, LANES), jnp.float32),
        ],
        scratch_shapes=[
            pltpu.VMEM((PEERS, rows, width), jnp.bfloat16),
            pltpu.VMEM((PEERS, NOTE, width), jnp.bfloat16),
            pltpu.VMEM((2, rows, GROUP * width), jnp.bfloat16),
            pltpu.VMEM((AHEAD, GROUP * width, columns), jnp.bfloat16),
            pltpu.SemaphoreType.DMA((PEERS, 3)),
            pltpu.SemaphoreType.DMA((PEERS,)),
            pltpu.SemaphoreType.DMA((AHEAD, GROUP)),
        ],
        compiler_params=pltpu.CompilerParams(vmem_limit_bytes=HEAD_VMEM),
        name="head",
    )(*[blocks[key] for key in keys], weight)


def gate_kernel(tops_ref, scores_ref, kept_ref, mass_ref):
    parts = tops_ref.shape[1]
    top = rows_of([jnp.max(tops_ref[:, part, :], axis=0, keepdims=True) for part in range(parts)])
    shifted = scores_ref[...] - top[:, :1]
    kept = jnp.exp(shifted) * jax.nn.sigmoid(gate_sharpness * (shifted - min_p_log))
    kept_ref[...] = kept
    spread_rows(jnp.sum(kept, axis=1, keepdims=True), mass_ref)


def gate(tops, scores):
    return pl.pallas_call(
        gate_kernel,
        out_shape=[
            jax.ShapeDtypeStruct(scores.shape, jnp.float32),
            jax.ShapeDtypeStruct(tops.shape, jnp.float32),
        ],
        compiler_params=pltpu.CompilerParams(vmem_limit_bytes=SMALL_VMEM),
        name="gate",
    )(tops, scores)


def share_kernel(masses_ref, kept_ref, probs_ref):
    parts = masses_ref.shape[1]
    mass = rows_of(
        [jnp.sum(masses_ref[:, part, :], axis=0, keepdims=True) for part in range(parts)]
    )
    probs_ref[...] = kept_ref[...] / mass[:, :1]


def share(masses, kept):
    return pl.pallas_call(
        share_kernel,
        out_shape=jax.ShapeDtypeStruct(kept.shape, jnp.float32),
        compiler_params=pltpu.CompilerParams(vmem_limit_bytes=SMALL_VMEM),
        name="share",
    )(masses, kept)


def local(hidden, norm_gain, head_weight):
    micro, rows, width = hidden.shape
    blocks = {}

    def keep(name, value):
        blocks[0, name] = value
        blocks[1, name] = fetch(value, 0, 0, 1)
        return value

    note = jnp.pad(norm_gain[None], ((0, NOTE - 1), (0, 0)))
    own = keep("own", jnp.concatenate([note, hidden.reshape(micro * rows, width)], axis=0))
    left, right = keep("left", fetch(own, 0, -1)), keep("right", fetch(own, 0, 1))
    down, up = keep("down", fetch(own, -1, 0)), keep("up", fetch(own, 1, 0))
    cross_a = keep("cross_a", fetch(left[:TOP], 0, -1))
    cross_b = keep("cross_b", fetch(right[TOP:], 0, 1))
    over_a = keep("over_a", fetch(down[:TOP], -1, 0))
    over_b = keep("over_b", fetch(up[TOP:], 1, 0))

    row = jnp.concatenate([left[:TOP], right[:TOP], cross_a], axis=0)
    column = jnp.concatenate([down[TOP:], up[TOP:], over_b], axis=0)
    row, column, cross_b, over_a = lax.optimization_barrier((row, column, cross_b, over_a))
    row_down, row_up = keep("row_down", fetch(row, -1, 0)), keep("row_up", fetch(row, 1, 0))
    col_left, col_right = (
        keep("col_left", fetch(column, 0, -1)),
        keep("col_right", fetch(column, 0, 1)),
    )
    keep("far_down", fetch(row_down[:ROW_CUT], -1, 0))
    keep("far_up", fetch(row_up[ROW_CUT:], 1, 0))
    keep("far_left", fetch(col_left[:COLUMN_CUT], 0, -1))
    keep("far_right", fetch(col_right[COLUMN_CUT:], 0, 1))
    scores, logits, tops = head(blocks, head_weight)

    kept, masses = gate(exchange(tops), scores)
    probs = share(exchange(masses), kept)
    shape = (micro, rows, head_weight.shape[1])
    return logits.reshape(shape), probs.reshape(shape)


def solution(mesh):
    return jax.shard_map(
        local,
        mesh=mesh,
        in_specs=(
            P("dp", None, AXES),
            P(AXES),
            P(None, AXES),
        ),
        out_specs=(P("dp", None, AXES), P("dp", None, AXES)),
        check_vma=False,
    )
```

time: 120 us -> 105 us (0.88)
  starting transfers between devices: 0.04 us -> 35.8 us
  waiting for transfers between devices: 41.3 us -> 19.2 us
  blocking collectives: 39.3 us -> 21.9 us
  between operations: 14.1 us -> 1.11 us
  local copies, waits for them, and re-layouts: 0.31 us -> 3.42 us
    all_gather x1 -> x0, waiting for transfers between devices: 40.6 us -> none  [local(): pieces = lax.all_gather(flat, AXES, axis=0)]
    ppermute x0 -> x33, starting transfers between devices: none -> 35.8 us  [fetch(): return lax.ppermute(value, AXES, pairs)]
    ppermute x0 -> x33, waiting for transfers between devices: none -> 19.2 us  [fetch(): return lax.ppermute(value, AXES, pairs)]
    all_to_all x3 -> x2, blocking collectives: 39.3 us -> 21.9 us  [exchange(): return lax.all_to_all(values, AXES, 0, 0, tiled=True)]
    unnamed x1 -> x70, local copies, waits for them, and re-layouts: 0.02 us -> 2.62 us
  transfers between devices with their start and end apart: 1 -> 33, of which waited for: 1 -> 10; matrix products, arithmetic and copies ran while one was open for 2% -> 0% of each run, Pallas kernels for 0% -> 0%
where the time goes in v2:
time: 105 us
  starting transfers between devices  35.8 us (34%)
  Pallas kernels  22.7 us (22%)
  blocking collectives  21.9 us (21%)
  waiting for transfers between devices  19.2 us (18%)
  local copies, waits for them, and re-layouts  3.42 us (3%)
  between operations  1.11 us (1%)
    ppermute x33, starting transfers between devices, fetch(): return lax.ppermute(value, AXES, pairs)  35.8 us
    all_to_all x2, blocking collectives, exchange(): return lax.all_to_all(values, AXES, 0, 0, tiled=True)  21.9 us
    pallas_call x1, Pallas kernels, head(): pl.pallas_call(functools.partial(head_kernel, keys), in_specs=[pl.BlockSp...  21.1 us
    ppermute x33, waiting for transfers between devices, fetch(): return lax.ppermute(value, AXES, pairs)  19.2 us
    unnamed x70, local copies, waits for them, and re-layouts  2.62 us
  transfers between devices with their start and end apart: 33, of which 10 were waited for; matrix products, arithmetic and copies ran while one was open for 0% of the time, Pallas kernels for 0%

profile of v2, /device:TPU:1, one launch (start us, length us, event | category | flops | bytes accessed | tf_op | source)
XLA Modules:
  0.0 105.1 jit_solution(16050705134222338676)
XLA Ops:
  1.3 1.0 fusion.1.refs_0_
  2.3 3.6 %collective-permute-start.3 = (bf16[272,512]{1,0:T(8,128)(2,1)S(1)}, bf16[272,512]{1,0:T(8,128)(2,1)S(1)}, u32[]{:S(2)}, u32[]{:S(2)}) collective-permute-start(bf16[272,512]{1,0:T(8,128)(2,1)S(1)} %fusion.1.refs_0_), channel_id=1, source_target_pairs={{32,0},{36,4},{40,8},{44,12},{48,16},{52,20},{56,24},{60,28},{64,3... | collective-permute-start | bytes 835592 | tf_op jit(solution)/shard_map/ppermute | solution.py:69
  5.9 1.2 %collective-permute-start = (bf16[272,512]{1,0:T(8,128)(2,1)S(1)}, bf16[272,512]{1,0:T(8,128)(2,1)S(1)}, u32[]{:S(2)}, u32[]{:S(2)}) collective-permute-start(bf16[272,512]{1,0:T(8,128)(2,1)S(1)} %fusion.1.refs_0_), channel_id=1, source_target_pairs={{24,0},{28,4},{0,8},{4,12},{8,16},{12,20},{16,24},{20,28},{56,32},... | collective-permute-start | bytes 835592 | tf_op jit(solution)/shard_map/ppermute | solution.py:69
  7.1 1.5 %collective-permute-start.1 = (bf16[272,512]{1,0:T(8,128)(2,1)S(1)}, bf16[272,512]{1,0:T(8,128)(2,1)S(1)}, u32[]{:S(2)}, u32[]{:S(2)}) collective-permute-start(bf16[272,512]{1,0:T(8,128)(2,1)S(1)} %fusion.1.refs_0_), channel_id=1, source_target_pairs={{8,0},{12,4},{16,8},{20,12},{24,16},{28,20},{0,24},{4,28},{40,32},... | collective-permute-start | bytes 835592 | tf_op jit(solution)/shard_map/ppermute | solution.py:69
  8.6 2.6 %collective-permute-done.3.refs_4_ = bf16[272,512]{1,0:T(8,128)(2,1)S(1)} collective-permute-done((bf16[272,512]{1,0:T(8,128)(2,1)S(1)}, bf16[272,512]{1,0:T(8,128)(2,1)S(1)}, u32[]{:S(2)}, u32[]{:S(2)}) %collective-permute-start.3) | collective-permute-done | bytes 278560 | tf_op jit(solution)/shard_map/ppermute | solution.py:69
  11.3 3.5 %collective-permute-start.7 = (bf16[128,512]{1,0:T(8,128)(2,1)S(1)}, bf16[128,512]{1,0:T(8,128)(2,1)S(1)}, u32[]{:S(2)}, u32[]{:S(2)}) collective-permute-start(bf16[128,512]{1,0:T(8,128)(2,1)S(1)} %slice.45), channel_id=1, source_target_pairs={{32,0},{36,4},{40,8},{44,12},{48,16},{52,20},{56,24},{60,28},{64,3... | collective-permute-start | bytes 393224 | tf_op jit(solution)/shard_map/ppermute | solution.py:69
  14.7 1.8 %collective-permute-start.16 = (bf16[272,512]{1,0:T(8,128)(2,1)S(1)}, bf16[272,512]{1,0:T(8,128)(2,1)S(1)}, u32[]{:S(2)}, u32[]{:S(2)}) collective-permute-start(bf16[272,512]{1,0:T(8,128)(2,1)S(1)} %fusion.1.refs_0_), channel_id=1, source_target_pairs={{4,0},{0,4},{12,8},{8,12},{20,16},{16,20},{28,24},{24,28},{36,32},... | collective-permute-start | bytes 835592 | tf_op jit(solution)/shard_map/ppermute | solution.py:69
  16.6 1.3 %collective-permute-start.4 = (bf16[144,512]{1,0:T(8,128)(2,1)S(1)}, bf16[144,512]{1,0:T(8,128)(2,1)S(1)}, u32[]{:S(2)}, u32[]{:S(2)}) collective-permute-start(bf16[144,512]{1,0:T(8,128)(2,1)S(1)} %slice.42), channel_id=1, source_target_pairs={{24,0},{28,4},{0,8},{4,12},{8,16},{12,20},{16,24},{20,28},{56,32},... | collective-permute-start | bytes 442376 | tf_op jit(solution)/shard_map/ppermute | solution.py:69
  17.9 1.5 %collective-permute-start.5 = (bf16[128,512]{1,0:T(8,128)(2,1)S(1)}, bf16[128,512]{1,0:T(8,128)(2,1)S(1)}, u32[]{:S(2)}, u32[]{:S(2)}) collective-permute-start(bf16[128,512]{1,0:T(8,128)(2,1)S(1)} %slice.43), channel_id=1, source_target_pairs={{8,0},{12,4},{16,8},{20,12},{24,16},{28,20},{0,24},{4,28},{40,32},... | collective-permute-start | bytes 393224 | tf_op jit(solution)/shard_map/ppermute | solution.py:69
  20.3 2.5 %collective-permute-done.5.refs_6_ = bf16[128,512]{1,0:T(8,128)(2,1)S(1)} collective-permute-done((bf16[128,512]{1,0:T(8,128)(2,1)S(1)}, bf16[128,512]{1,0:T(8,128)(2,1)S(1)}, u32[]{:S(2)}, u32[]{:S(2)}) %collective-permute-start.5) | collective-permute-done | bytes 131104 | tf_op jit(solution)/shard_map/ppermute | solution.py:69
  22.8 1.1 %collective-permute-start.19 = (bf16[272,512]{1,0:T(8,128)(2,1)S(1)}, bf16[272,512]{1,0:T(8,128)(2,1)S(1)}, u32[]{:S(2)}, u32[]{:S(2)}) collective-permute-start(bf16[272,512]{1,0:T(8,128)(2,1)S(1)} %collective-permute-done.2.refs_3_), channel_id=1, source_target_pairs={{4,0},{0,4},{12,8},{8,12},{20,16},{16,20},{28,24},{24,28},{36,32},... | collective-permute-start | bytes 835592 | tf_op jit(solution)/shard_map/ppermute | solution.py:69
  24.2 1.4 %collective-permute-done.6.refs_7_ = bf16[144,512]{1,0:T(8,128)(2,1)S(1)} collective-permute-done((bf16[144,512]{1,0:T(8,128)(2,1)S(1)}, bf16[144,512]{1,0:T(8,128)(2,1)S(1)}, u32[]{:S(2)}, u32[]{:S(2)}) %collective-permute-start.6) | collective-permute-done | bytes 147488 | tf_op jit(solution)/shard_map/ppermute | solution.py:69
  25.6 1.3 %collective-permute-start.10 = (bf16[384,512]{1,0:T(8,128)(2,1)S(1)}, bf16[384,512]{1,0:T(8,128)(2,1)S(1)}, u32[]{:S(2)}, u32[]{:S(2)}) collective-permute-start(bf16[384,512]{1,0:T(8,128)(2,1)S(1)} %pad_maximum_fusion.1), channel_id=1, source_target_pairs={{8,0},{12,4},{16,8},{20,12},{24,16},{28,20},{0,24},{4,28},{40,32},... | collective-permute-start | bytes 1179656 | tf_op jit(solution)/shard_map/ppermute | solution.py:69
  26.8 1.7 %collective-permute-start.22 = (bf16[128,512]{1,0:T(8,128)(2,1)S(1)}, bf16[128,512]{1,0:T(8,128)(2,1)S(1)}, u32[]{:S(2)}, u32[]{:S(2)}) collective-permute-start(bf16[128,512]{1,0:T(8,128)(2,1)S(1)} %collective-permute-done.5.refs_6_), channel_id=1, source_target_pairs={{4,0},{0,4},{12,8},{8,12},{20,16},{16,20},{28,24},{24,28},{36,32},... | collective-permute-start | bytes 393224 | tf_op jit(solution)/shard_map/ppermute | solution.py:69
  28.6 1.0 collective-permute-done.22.refs_23_
  29.7 1.7 %collective-permute-start.12 = (bf16[432,512]{1,0:T(8,128)(2,1)S(1)}, bf16[432,512]{1,0:T(8,128)(2,1)S(1)}, u32[]{:S(2)}, u32[]{:S(2)}) collective-permute-start(bf16[432,512]{1,0:T(8,128)(2,1)S(1)} %pad_maximum_fusion), channel_id=1, source_target_pairs={{32,0},{36,4},{40,8},{44,12},{48,16},{52,20},{56,24},{60,28},{64,3... | collective-permute-start | bytes 1327112 | tf_op jit(solution)/shard_map/ppermute | solution.py:69
  31.5 0.9 collective-permute-start.18
  32.4 2.4 %collective-permute-done.10.refs_11_ = bf16[384,512]{1,0:T(8,128)(2,1)S(1)} collective-permute-done((bf16[384,512]{1,0:T(8,128)(2,1)S(1)}, bf16[384,512]{1,0:T(8,128)(2,1)S(1)}, u32[]{:S(2)}, u32[]{:S(2)}) %collective-permute-start.10) | collective-permute-done | bytes 393248 | tf_op jit(solution)/shard_map/ppermute | solution.py:69
  34.8 2.3 %collective-permute-start.17 = (bf16[272,512]{1,0:T(8,128)(2,1)S(1)}, bf16[272,512]{1,0:T(8,128)(2,1)S(1)}, u32[]{:S(2)}, u32[]{:S(2)}) collective-permute-start(bf16[272,512]{1,0:T(8,128)(2,1)S(1)} %collective-permute-done.refs_1_), channel_id=1, source_target_pairs={{4,0},{0,4},{12,8},{8,12},{20,16},{16,20},{28,24},{24,28},{36,32},... | collective-permute-start | bytes 835592 | tf_op jit(solution)/shard_map/ppermute | solution.py:69
  37.1 2.5 %collective-permute-start.13 = (bf16[192,512]{1,0:T(8,128)(2,1)S(1)}, bf16[192,512]{1,0:T(8,128)(2,1)S(1)}, u32[]{:S(2)}, u32[]{:S(2)}) collective-permute-start(bf16[192,512]{1,0:T(8,128)(2,1)S(1)} %slice.49), channel_id=1, source_target_pairs={{8,0},{12,4},{16,8},{20,12},{24,16},{28,20},{0,24},{4,28},{40,32},... | collective-permute-start | bytes 589832 | tf_op jit(solution)/shard_map/ppermute | solution.py:69
  39.7 1.4 %collective-permute-done.9.refs_10_ = bf16[384,512]{1,0:T(8,128)(2,1)S(1)} collective-permute-done((bf16[384,512]{1,0:T(8,128)(2,1)S(1)}, bf16[384,512]{1,0:T(8,128)(2,1)S(1)}, u32[]{:S(2)}, u32[]{:S(2)}) %collective-permute-start.9) | collective-permute-done | bytes 393248 | tf_op jit(solution)/shard_map/ppermute | solution.py:69
  41.1 1.2 %collective-permute-start.23 = (bf16[144,512]{1,0:T(8,128)(2,1)S(1)}, bf16[144,512]{1,0:T(8,128)(2,1)S(1)}, u32[]{:S(2)}, u32[]{:S(2)}) collective-permute-start(bf16[144,512]{1,0:T(8,128)(2,1)S(1)} %collective-permute-done.6.refs_7_), channel_id=1, source_target_pairs={{4,0},{0,4},{12,8},{8,12},{20,16},{16,20},{28,24},{24,28},{36,32},... | collective-permute-start | bytes 442376 | tf_op jit(solution)/shard_map/ppermute | solution.py:69
  42.6 2.7 %collective-permute-start.15 = (bf16[224,512]{1,0:T(8,128)(2,1)S(1)}, bf16[224,512]{1,0:T(8,128)(2,1)S(1)}, u32[]{:S(2)}, u32[]{:S(2)}) collective-permute-start(bf16[224,512]{1,0:T(8,128)(2,1)S(1)} %slice.51), channel_id=1, source_target_pairs={{32,0},{36,4},{40,8},{44,12},{48,16},{52,20},{56,24},{60,28},{64,3... | collective-permute-start | bytes 688136 | tf_op jit(solution)/shard_map/ppermute | solution.py:69
  46.5 5.4 %collective-permute-done.11.refs_12_ = bf16[192,512]{1,0:T(8,128)(2,1)S(1)} collective-permute-done((bf16[192,512]{1,0:T(8,128)(2,1)S(1)}, bf16[192,512]{1,0:T(8,128)(2,1)S(1)}, u32[]{:S(2)}, u32[]{:S(2)}) %collective-permute-start.11) | collective-permute-done | bytes 196640 | tf_op jit(solution)/shard_map/ppermute | solution.py:69
  51.9 1.9 %collective-permute-start.29 = (bf16[432,512]{1,0:T(8,128)(2,1)S(1)}, bf16[432,512]{1,0:T(8,128)(2,1)S(1)}, u32[]{:S(2)}, u32[]{:S(2)}) collective-permute-start(bf16[432,512]{1,0:T(8,128)(2,1)S(1)} %collective-permute-done.12.refs_13_), channel_id=1, source_target_pairs={{4,0},{0,4},{12,8},{8,12},{20,16},{16,20},{28,24},{24,28},{36,32},... | collective-permute-start | bytes 1327112 | tf_op jit(solution)/shard_map/ppermute | solution.py:69
  54.9 1.3 %collective-permute-done.28.refs_29_ = bf16[192,512]{1,0:T(8,128)(2,1)S(1)} collective-permute-done((bf16[192,512]{1,0:T(8,128)(2,1)S(1)}, bf16[192,512]{1,0:T(8,128)(2,1)S(1)}, u32[]{:S(2)}, u32[]{:S(2)}) %collective-permute-start.28) | collective-permute-done | bytes 196640 | tf_op jit(solution)/shard_map/ppermute | solution.py:69
  56.7 0.9 collective-permute-done.31.refs_32_
  59.3 21.1 %head.1 = (f32[256,768]{1,0:T(8,128)}, bf16[256,768]{1,0:T(8,128)(2,1)}, f32[32,2,128]{2,1,0:T(2,128)}) custom-call(bf16[272,512]{1,0:T(8,128)(2,1)} %copy-done.1, bf16[272,512]{1,0:T(8,128)(2,1)} %copy-done.8, bf16[272,512]{1,0:T(8,128)(2,1)} %copy-done.2, bf16[272,512]{1,0:T(8,128)(2,1)} %copy-done.3, bf16[272,512]{1,0:T(8,128)(2,1)} %copy-done.9, ...), custom_call_target="tpu_custom_call" | custom-call | tf_op jit(solution)/shard_map/head/pallas_call | solution.py:188
  80.4 11.2 %all_to_all.10.tops_ref = f32[32,2,128]{2,1,0:T(2,128)S(1)} all-to-all(f32[32,2,128]{2,1,0:T(2,128)} %get-tuple-element.12), channel_id=1, replica_groups=mesh['pipe'=4,'tensor'=8,'dp'=4] {'pipe','tensor'}, dimensions={0} | all-to-all | bytes 65536 | tf_op jit(solution)/shard_map/all_to_all | solution.py:73
  91.6 1.1 %copy-done = f32[256,768]{1,0:T(8,128)S(1)} copy-done((f32[256,768]{1,0:T(8,128)S(1)}, f32[256,768]{1,0:T(8,128)}, u32[]{:S(2)}) %copy-start) | copy-done | bytes 786456
  93.3 10.7 %all_to_all.11.masses_ref = f32[32,2,128]{2,1,0:T(2,128)S(1)} all-to-all(f32[32,2,128]{2,1,0:T(2,128)S(1)} %get-tuple-element.14), channel_id=1, replica_groups=mesh['pipe'=4,'tensor'=8,'dp'=4] {'pipe','tensor'}, dimensions={0} | all-to-all | bytes 65536 | tf_op jit(solution)/shard_map/all_to_all | solution.py:73
  104.0 1.1 %share.1 = f32[256,768]{1,0:T(8,128)} custom-call(f32[32,2,128]{2,1,0:T(2,128)S(1)} %all_to_all.11.masses_ref, f32[256,768]{1,0:T(8,128)S(1)} %get-tuple-element.15.kept_ref), custom_call_target="tpu_custom_call" | custom-call | tf_op jit(solution)/shard_map/share/pallas_call | solution.py:241
  (123 shorter events, 7.1 us)
Async XLA Ops:
  2.3 9.0 %collective-permute-start.3 = (bf16[272,512]{1,0:T(8,128)(2,1)S(1)}, bf16[272,512]{1,0:T(8,128)(2,1)S(1)}, u32[]{:S(2)}, u32[]{:S(2)}) collective-permute-start(bf16[272,512]{1,0:T(8,128)(2,1)S(1)} %fusion.1.refs_0_), channel_id=1, source_target_pairs={{32,0},{36,4},{40,8},{44,12},{48,16},{52,20},{56,24},{60,28},{64,3... | collective-permute-start | bytes 835592 | tf_op jit(solution)/shard_map/ppermute | solution.py:69
  5.9 10.7 %collective-permute-start = (bf16[272,512]{1,0:T(8,128)(2,1)S(1)}, bf16[272,512]{1,0:T(8,128)(2,1)S(1)}, u32[]{:S(2)}, u32[]{:S(2)}) collective-permute-start(bf16[272,512]{1,0:T(8,128)(2,1)S(1)} %fusion.1.refs_0_), channel_id=1, source_target_pairs={{24,0},{28,4},{0,8},{4,12},{8,16},{12,20},{16,24},{20,28},{56,32},... | collective-permute-start | bytes 835592 | tf_op jit(solution)/shard_map/ppermute | solution.py:69
  7.1 10.7 %collective-permute-start.1 = (bf16[272,512]{1,0:T(8,128)(2,1)S(1)}, bf16[272,512]{1,0:T(8,128)(2,1)S(1)}, u32[]{:S(2)}, u32[]{:S(2)}) collective-permute-start(bf16[272,512]{1,0:T(8,128)(2,1)S(1)} %fusion.1.refs_0_), channel_id=1, source_target_pairs={{8,0},{12,4},{16,8},{20,12},{24,16},{28,20},{0,24},{4,28},{40,32},... | collective-permute-start | bytes 835592 | tf_op jit(solution)/shard_map/ppermute | solution.py:69
  8.6 10.8 %collective-permute-start.2 = (bf16[272,512]{1,0:T(8,128)(2,1)S(1)}, bf16[272,512]{1,0:T(8,128)(2,1)S(1)}, u32[]{:S(2)}, u32[]{:S(2)}) collective-permute-start(bf16[272,512]{1,0:T(8,128)(2,1)S(1)} %fusion.1.refs_0_), channel_id=1, source_target_pairs={{96,0},{100,4},{104,8},{108,12},{112,16},{116,20},{120,24},{124,28... | collective-permute-start | bytes 835592 | tf_op jit(solution)/shard_map/ppermute | solution.py:69
  11.3 8.3 %collective-permute-start.7 = (bf16[128,512]{1,0:T(8,128)(2,1)S(1)}, bf16[128,512]{1,0:T(8,128)(2,1)S(1)}, u32[]{:S(2)}, u32[]{:S(2)}) collective-permute-start(bf16[128,512]{1,0:T(8,128)(2,1)S(1)} %slice.45), channel_id=1, source_target_pairs={{32,0},{36,4},{40,8},{44,12},{48,16},{52,20},{56,24},{60,28},{64,3... | collective-permute-start | bytes 393224 | tf_op jit(solution)/shard_map/ppermute | solution.py:69
  14.7 12.1 %collective-permute-start.16 = (bf16[272,512]{1,0:T(8,128)(2,1)S(1)}, bf16[272,512]{1,0:T(8,128)(2,1)S(1)}, u32[]{:S(2)}, u32[]{:S(2)}) collective-permute-start(bf16[272,512]{1,0:T(8,128)(2,1)S(1)} %fusion.1.refs_0_), channel_id=1, source_target_pairs={{4,0},{0,4},{12,8},{8,12},{20,16},{16,20},{28,24},{24,28},{36,32},... | collective-permute-start | bytes 835592 | tf_op jit(solution)/shard_map/ppermute | solution.py:69
  16.6 7.3 %collective-permute-start.4 = (bf16[144,512]{1,0:T(8,128)(2,1)S(1)}, bf16[144,512]{1,0:T(8,128)(2,1)S(1)}, u32[]{:S(2)}, u32[]{:S(2)}) collective-permute-start(bf16[144,512]{1,0:T(8,128)(2,1)S(1)} %slice.42), channel_id=1, source_target_pairs={{24,0},{28,4},{0,8},{4,12},{8,16},{12,20},{16,24},{20,28},{56,32},... | collective-permute-start | bytes 442376 | tf_op jit(solution)/shard_map/ppermute | solution.py:69
  17.9 4.9 %collective-permute-start.5 = (bf16[128,512]{1,0:T(8,128)(2,1)S(1)}, bf16[128,512]{1,0:T(8,128)(2,1)S(1)}, u32[]{:S(2)}, u32[]{:S(2)}) collective-permute-start(bf16[128,512]{1,0:T(8,128)(2,1)S(1)} %slice.43), channel_id=1, source_target_pairs={{8,0},{12,4},{16,8},{20,12},{24,16},{28,20},{0,24},{4,28},{40,32},... | collective-permute-start | bytes 393224 | tf_op jit(solution)/shard_map/ppermute | solution.py:69
  19.5 6.1 %collective-permute-start.6 = (bf16[144,512]{1,0:T(8,128)(2,1)S(1)}, bf16[144,512]{1,0:T(8,128)(2,1)S(1)}, u32[]{:S(2)}, u32[]{:S(2)}) collective-permute-start(bf16[144,512]{1,0:T(8,128)(2,1)S(1)} %slice.44), channel_id=1, source_target_pairs={{96,0},{100,4},{104,8},{108,12},{112,16},{116,20},{120,24},{124,28... | collective-permute-start | bytes 442376 | tf_op jit(solution)/shard_map/ppermute | solution.py:69
  19.6 10.1 %collective-permute-start.20 = (bf16[272,512]{1,0:T(8,128)(2,1)S(1)}, bf16[272,512]{1,0:T(8,128)(2,1)S(1)}, u32[]{:S(2)}, u32[]{:S(2)}) collective-permute-start(bf16[272,512]{1,0:T(8,128)(2,1)S(1)} %collective-permute-done.3.refs_4_), channel_id=1, source_target_pairs={{4,0},{0,4},{12,8},{8,12},{20,16},{16,20},{28,24},{24,28},{36,32},... | collective-permute-start | bytes 835592 | tf_op jit(solution)/shard_map/ppermute | solution.py:69
  22.8 8.7 %collective-permute-start.19 = (bf16[272,512]{1,0:T(8,128)(2,1)S(1)}, bf16[272,512]{1,0:T(8,128)(2,1)S(1)}, u32[]{:S(2)}, u32[]{:S(2)}) collective-permute-start(bf16[272,512]{1,0:T(8,128)(2,1)S(1)} %collective-permute-done.2.refs_3_), channel_id=1, source_target_pairs={{4,0},{0,4},{12,8},{8,12},{20,16},{16,20},{28,24},{24,28},{36,32},... | collective-permute-start | bytes 835592 | tf_op jit(solution)/shard_map/ppermute | solution.py:69
  23.9 4.7 %collective-permute-start.24 = (bf16[128,512]{1,0:T(8,128)(2,1)S(1)}, bf16[128,512]{1,0:T(8,128)(2,1)S(1)}, u32[]{:S(2)}, u32[]{:S(2)}) collective-permute-start(bf16[128,512]{1,0:T(8,128)(2,1)S(1)} %collective-permute-done.7.refs_8_), channel_id=1, source_target_pairs={{4,0},{0,4},{12,8},{8,12},{20,16},{16,20},{28,24},{24,28},{36,32},... | collective-permute-start | bytes 393224 | tf_op jit(solution)/shard_map/ppermute | solution.py:69
  25.6 9.2 %collective-permute-start.10 = (bf16[384,512]{1,0:T(8,128)(2,1)S(1)}, bf16[384,512]{1,0:T(8,128)(2,1)S(1)}, u32[]{:S(2)}, u32[]{:S(2)}) collective-permute-start(bf16[384,512]{1,0:T(8,128)(2,1)S(1)} %pad_maximum_fusion.1), channel_id=1, source_target_pairs={{8,0},{12,4},{16,8},{20,12},{24,16},{28,20},{0,24},{4,28},{40,32},... | collective-permute-start | bytes 1179656 | tf_op jit(solution)/shard_map/ppermute | solution.py:69
  26.8 2.7 %collective-permute-start.22 = (bf16[128,512]{1,0:T(8,128)(2,1)S(1)}, bf16[128,512]{1,0:T(8,128)(2,1)S(1)}, u32[]{:S(2)}, u32[]{:S(2)}) collective-permute-start(bf16[128,512]{1,0:T(8,128)(2,1)S(1)} %collective-permute-done.5.refs_6_), channel_id=1, source_target_pairs={{4,0},{0,4},{12,8},{8,12},{20,16},{16,20},{28,24},{24,28},{36,32},... | collective-permute-start | bytes 393224 | tf_op jit(solution)/shard_map/ppermute | solution.py:69
  28.6 13.7 %collective-permute-start.8 = (bf16[432,512]{1,0:T(8,128)(2,1)S(1)}, bf16[432,512]{1,0:T(8,128)(2,1)S(1)}, u32[]{:S(2)}, u32[]{:S(2)}) collective-permute-start(bf16[432,512]{1,0:T(8,128)(2,1)S(1)} %pad_maximum_fusion), channel_id=1, source_target_pairs={{96,0},{100,4},{104,8},{108,12},{112,16},{116,20},{120,24},{124,28... | collective-permute-start | bytes 1327112 | tf_op jit(solution)/shard_map/ppermute | solution.py:69
  29.5 11.6 %collective-permute-start.9 = (bf16[384,512]{1,0:T(8,128)(2,1)S(1)}, bf16[384,512]{1,0:T(8,128)(2,1)S(1)}, u32[]{:S(2)}, u32[]{:S(2)}) collective-permute-start(bf16[384,512]{1,0:T(8,128)(2,1)S(1)} %pad_maximum_fusion.1), channel_id=1, source_target_pairs={{24,0},{28,4},{0,8},{4,12},{8,16},{12,20},{16,24},{20,28},{56,32},... | collective-permute-start | bytes 1179656 | tf_op jit(solution)/shard_map/ppermute | solution.py:69
  29.7 12.7 %collective-permute-start.12 = (bf16[432,512]{1,0:T(8,128)(2,1)S(1)}, bf16[432,512]{1,0:T(8,128)(2,1)S(1)}, u32[]{:S(2)}, u32[]{:S(2)}) collective-permute-start(bf16[432,512]{1,0:T(8,128)(2,1)S(1)} %pad_maximum_fusion), channel_id=1, source_target_pairs={{32,0},{36,4},{40,8},{44,12},{48,16},{52,20},{56,24},{60,28},{64,3... | collective-permute-start | bytes 1327112 | tf_op jit(solution)/shard_map/ppermute | solution.py:69
  31.5 5.7 %collective-permute-start.18 = (bf16[272,512]{1,0:T(8,128)(2,1)S(1)}, bf16[272,512]{1,0:T(8,128)(2,1)S(1)}, u32[]{:S(2)}, u32[]{:S(2)}) collective-permute-start(bf16[272,512]{1,0:T(8,128)(2,1)S(1)} %collective-permute-done.1.refs_2_), channel_id=1, source_target_pairs={{4,0},{0,4},{12,8},{8,12},{20,16},{16,20},{28,24},{24,28},{36,32},... | collective-permute-start | bytes 835592 | tf_op jit(solution)/shard_map/ppermute | solution.py:69
  34.8 7.8 %collective-permute-start.17 = (bf16[272,512]{1,0:T(8,128)(2,1)S(1)}, bf16[272,512]{1,0:T(8,128)(2,1)S(1)}, u32[]{:S(2)}, u32[]{:S(2)}) collective-permute-start(bf16[272,512]{1,0:T(8,128)(2,1)S(1)} %collective-permute-done.refs_1_), channel_id=1, source_target_pairs={{4,0},{0,4},{12,8},{8,12},{20,16},{16,20},{28,24},{24,28},{36,32},... | collective-permute-start | bytes 835592 | tf_op jit(solution)/shard_map/ppermute | solution.py:69
  37.1 9.2 %collective-permute-start.13 = (bf16[192,512]{1,0:T(8,128)(2,1)S(1)}, bf16[192,512]{1,0:T(8,128)(2,1)S(1)}, u32[]{:S(2)}, u32[]{:S(2)}) collective-permute-start(bf16[192,512]{1,0:T(8,128)(2,1)S(1)} %slice.49), channel_id=1, source_target_pairs={{8,0},{12,4},{16,8},{20,12},{24,16},{28,20},{0,24},{4,28},{40,32},... | collective-permute-start | bytes 589832 | tf_op jit(solution)/shard_map/ppermute | solution.py:69
  41.1 4.2 %collective-permute-start.23 = (bf16[144,512]{1,0:T(8,128)(2,1)S(1)}, bf16[144,512]{1,0:T(8,128)(2,1)S(1)}, u32[]{:S(2)}, u32[]{:S(2)}) collective-permute-start(bf16[144,512]{1,0:T(8,128)(2,1)S(1)} %collective-permute-done.6.refs_7_), channel_id=1, source_target_pairs={{4,0},{0,4},{12,8},{8,12},{20,16},{16,20},{28,24},{24,28},{36,32},... | collective-permute-start | bytes 442376 | tf_op jit(solution)/shard_map/ppermute | solution.py:69
  42.3 3.2 %collective-permute-start.21 = (bf16[144,512]{1,0:T(8,128)(2,1)S(1)}, bf16[144,512]{1,0:T(8,128)(2,1)S(1)}, u32[]{:S(2)}, u32[]{:S(2)}) collective-permute-start(bf16[144,512]{1,0:T(8,128)(2,1)S(1)} %collective-permute-done.4.refs_5_), channel_id=1, source_target_pairs={{4,0},{0,4},{12,8},{8,12},{20,16},{16,20},{28,24},{24,28},{36,32},... | collective-permute-start | bytes 442376 | tf_op jit(solution)/shard_map/ppermute | solution.py:69
  42.4 11.4 %collective-permute-start.14 = (bf16[208,512]{1,0:T(8,128)(2,1)S(1)}, bf16[208,512]{1,0:T(8,128)(2,1)S(1)}, u32[]{:S(2)}, u32[]{:S(2)}) collective-permute-start(bf16[208,512]{1,0:T(8,128)(2,1)S(1)} %slice.50), channel_id=1, source_target_pairs={{96,0},{100,4},{104,8},{108,12},{112,16},{116,20},{120,24},{124,28... | collective-permute-start | bytes 638984 | tf_op jit(solution)/shard_map/ppermute | solution.py:69
  42.6 11.4 %collective-permute-start.15 = (bf16[224,512]{1,0:T(8,128)(2,1)S(1)}, bf16[224,512]{1,0:T(8,128)(2,1)S(1)}, u32[]{:S(2)}, u32[]{:S(2)}) collective-permute-start(bf16[224,512]{1,0:T(8,128)(2,1)S(1)} %slice.51), channel_id=1, source_target_pairs={{32,0},{36,4},{40,8},{44,12},{48,16},{52,20},{56,24},{60,28},{64,3... | collective-permute-start | bytes 688136 | tf_op jit(solution)/shard_map/ppermute | solution.py:69
  45.3 6.6 %collective-permute-start.11 = (bf16[192,512]{1,0:T(8,128)(2,1)S(1)}, bf16[192,512]{1,0:T(8,128)(2,1)S(1)}, u32[]{:S(2)}, u32[]{:S(2)}) collective-permute-start(bf16[192,512]{1,0:T(8,128)(2,1)S(1)} %slice.48), channel_id=1, source_target_pairs={{24,0},{28,4},{0,8},{4,12},{8,16},{12,20},{16,24},{20,28},{56,32},... | collective-permute-start | bytes 589832 | tf_op jit(solution)/shard_map/ppermute | solution.py:69
  45.5 9.0 %collective-permute-start.27 = (bf16[384,512]{1,0:T(8,128)(2,1)S(1)}, bf16[384,512]{1,0:T(8,128)(2,1)S(1)}, u32[]{:S(2)}, u32[]{:S(2)}) collective-permute-start(bf16[384,512]{1,0:T(8,128)(2,1)S(1)} %collective-permute-done.10.refs_11_), channel_id=1, source_target_pairs={{4,0},{0,4},{12,8},{8,12},{20,16},{16,20},{28,24},{24,28},{36,32},... | collective-permute-start | bytes 1179656 | tf_op jit(solution)/shard_map/ppermute | solution.py:69
  46.4 8.0 %collective-permute-start.30 = (bf16[192,512]{1,0:T(8,128)(2,1)S(1)}, bf16[192,512]{1,0:T(8,128)(2,1)S(1)}, u32[]{:S(2)}, u32[]{:S(2)}) collective-permute-start(bf16[192,512]{1,0:T(8,128)(2,1)S(1)} %collective-permute-done.13.refs_14_), channel_id=1, source_target_pairs={{4,0},{0,4},{12,8},{8,12},{20,16},{16,20},{28,24},{24,28},{36,32},... | collective-permute-start | bytes 589832 | tf_op jit(solution)/shard_map/ppermute | solution.py:69
  51.9 5.7 %collective-permute-start.29 = (bf16[432,512]{1,0:T(8,128)(2,1)S(1)}, bf16[432,512]{1,0:T(8,128)(2,1)S(1)}, u32[]{:S(2)}, u32[]{:S(2)}) collective-permute-start(bf16[432,512]{1,0:T(8,128)(2,1)S(1)} %collective-permute-done.12.refs_13_), channel_id=1, source_target_pairs={{4,0},{0,4},{12,8},{8,12},{20,16},{16,20},{28,24},{24,28},{36,32},... | collective-permute-start | bytes 1327112 | tf_op jit(solution)/shard_map/ppermute | solution.py:69
  53.8 3.8 %collective-permute-start.25 = (bf16[432,512]{1,0:T(8,128)(2,1)S(1)}, bf16[432,512]{1,0:T(8,128)(2,1)S(1)}, u32[]{:S(2)}, u32[]{:S(2)}) collective-permute-start(bf16[432,512]{1,0:T(8,128)(2,1)S(1)} %collective-permute-done.8.refs_9_), channel_id=1, source_target_pairs={{4,0},{0,4},{12,8},{8,12},{20,16},{16,20},{28,24},{24,28},{36,32},... | collective-permute-start | bytes 1327112 | tf_op jit(solution)/shard_map/ppermute | solution.py:69
  53.9 2.2 %collective-permute-start.28 = (bf16[192,512]{1,0:T(8,128)(2,1)S(1)}, bf16[192,512]{1,0:T(8,128)(2,1)S(1)}, u32[]{:S(2)}, u32[]{:S(2)}) collective-permute-start(bf16[192,512]{1,0:T(8,128)(2,1)S(1)} %collective-permute-done.11.refs_12_), channel_id=1, source_target_pairs={{4,0},{0,4},{12,8},{8,12},{20,16},{16,20},{28,24},{24,28},{36,32},... | collective-permute-start | bytes 589832 | tf_op jit(solution)/shard_map/ppermute | solution.py:69
  54.4 2.4 %collective-permute-start.26 = (bf16[384,512]{1,0:T(8,128)(2,1)S(1)}, bf16[384,512]{1,0:T(8,128)(2,1)S(1)}, u32[]{:S(2)}, u32[]{:S(2)}) collective-permute-start(bf16[384,512]{1,0:T(8,128)(2,1)S(1)} %collective-permute-done.9.refs_10_), channel_id=1, source_target_pairs={{4,0},{0,4},{12,8},{8,12},{20,16},{16,20},{28,24},{24,28},{36,32},... | collective-permute-start | bytes 1179656 | tf_op jit(solution)/shard_map/ppermute | solution.py:69
  54.5 3.2 %collective-permute-start.32 = (bf16[224,512]{1,0:T(8,128)(2,1)S(1)}, bf16[224,512]{1,0:T(8,128)(2,1)S(1)}, u32[]{:S(2)}, u32[]{:S(2)}) collective-permute-start(bf16[224,512]{1,0:T(8,128)(2,1)S(1)} %collective-permute-done.15.refs_16_), channel_id=1, source_target_pairs={{4,0},{0,4},{12,8},{8,12},{20,16},{16,20},{28,24},{24,28},{36,32},... | collective-permute-start | bytes 688136 | tf_op jit(solution)/shard_map/ppermute | solution.py:69
  (36 other events, 676.2 us)

commit v3 on v2

v3 whole, which is shorter than its diff:
```python
import functools
import math

import jax
import jax.numpy as jnp
from jax import lax
from jax.experimental import pallas as pl
from jax.experimental.pallas import tpu as pltpu
from jax.sharding import PartitionSpec as P

AXES = ("pipe", "tensor")
RING = 4
CORES = 2
PEERS = RING * RING * CORES
LANES = 128
NOTE = 16
HALF = 128
GROUP = 4
min_p_log = math.log(0.1)
gate_sharpness = 4.0
HEAD_VMEM = 14 * 1024 * 1024
SMALL_VMEM = 8 * 1024 * 1024

WHOLE = NOTE + 2 * HALF
TOP = NOTE + HALF
PLACES = {
    (0, 0): [("own", 0), ("own", NOTE, 2 * HALF)],
    (0, -1): [("left", 0), ("left", NOTE, 2 * HALF)],
    (0, 1): [("right", 0), ("right", NOTE, 2 * HALF)],
    (-1, 0): [("down", 0), ("down", NOTE, 2 * HALF)],
    (1, 0): [("up", 0), ("up", NOTE, 2 * HALF)],
    (0, 2): [("cross", 0), ("cross", NOTE, 2 * HALF)],
    (2, 0): [("over", 0), ("over", NOTE, 2 * HALF)],
}
for _dy, _array in ((-1, "row_down"), (1, "row_up"), (2, "row_over")):
    for _at, _dx in enumerate((-1, 1, 2)):
        PLACES[_dy, _dx] = [(_array, _at * TOP), (_array, _at * TOP + NOTE, HALF)]
for _dx, _array in ((-1, "col_left"), (1, "col_right"), (2, "col_cross")):
    for _at, _dy in enumerate((-1, 1, 2)):
        PLACES[_dy, _dx].append((_array, _at * HALF, HALF))


def device(y, x, core):
    return (y % RING) * RING * CORES + (x % RING) * CORES + core


def fetch(value, dy, dx, core=0):
    pairs = [
        (device(y + dy, x + dx, c ^ core), device(y, x, c))
        for y in range(RING)
        for x in range(RING)
        for c in range(CORES)
    ]
    return lax.ppermute(value, AXES, pairs)


def exchange(values):
    return lax.all_to_all(values, AXES, 0, 0, tiled=True)


def spread_rows(column, out_ref):
    rows = column.shape[0]
    across = jnp.broadcast_to(column, (rows, LANES)).T
    for part in range(rows // LANES):
        out_ref[:, part, :] = across[: out_ref.shape[0], part * LANES : (part + 1) * LANES]


def rows_of(parts):
    across = jnp.concatenate(parts, axis=1)
    return jnp.broadcast_to(across, (LANES, across.shape[1])).T


def bring(weight):
    def kernel(weight_ref, out_ref, sem):
        copy = pltpu.make_async_copy(weight_ref, out_ref, sem)
        copy.start()
        copy.wait()

    return pl.pallas_call(
        kernel,
        in_specs=[pl.BlockSpec(memory_space=pl.ANY)],
        out_specs=pl.BlockSpec(memory_space=pltpu.VMEM),
        out_shape=jax.ShapeDtypeStruct(weight.shape, weight.dtype),
        scratch_shapes=[pltpu.SemaphoreType.DMA],
        compiler_params=pltpu.CompilerParams(vmem_limit_bytes=SMALL_VMEM),
        cost_estimate=pl.CostEstimate(
            flops=0, bytes_accessed=2 * weight.size * weight.dtype.itemsize, transcendentals=0
        ),
        name="bring",
    )(weight)


def head_kernel(keys, *refs):
    block_refs = dict(zip(keys, refs))
    weight_ref, scores_ref, logits_ref, top_ref, normed_ref = refs[len(keys) :]
    pipe, tensor = lax.axis_index("pipe"), lax.axis_index("tensor")
    chip_x, core = tensor // CORES, lax.rem(tensor, CORES)
    rows = scores_ref.shape[0]
    width = weight_ref.shape[0] // PEERS
    terms = [(chip, which) for chip in PLACES for which in range(CORES)]
    groups = len(terms) // GROUP

    def runs(term):
        chip, which = terms[term]
        at = 0
        for array, start, count in PLACES[chip][1:]:
            yield slice(at, at + count), block_refs[which, array].at[pl.ds(start, count), :]
            at += count

    def gain_of(term):
        chip, which = terms[term]
        array, start = PLACES[chip][0]
        return block_refs[which, array][start : start + NOTE, :].astype(jnp.float32)[:1]

    squares = []
    for half in range(2):
        total = jnp.zeros((HALF, LANES), jnp.float32)
        for term in range(len(terms)):
            parts = []
            for at, ref in runs(term):
                first, last = max(at.start, half * HALF), min(at.stop, (half + 1) * HALF)
                if first < last:
                    parts.append(
                        sum(
                            jnp.square(
                                ref[
                                    first - at.start : last - at.start, lane : lane + LANES
                                ].astype(jnp.float32)
                            )
                            for lane in range(0, width, LANES)
                        )
                    )
            total += parts[0] if len(parts) == 1 else jnp.concatenate(parts, axis=0)
        squares.append(jnp.sum(total, axis=1, keepdims=True))
    total_sq = jnp.concatenate(squares, axis=0)
    scale = lax.rsqrt(total_sq / (width * len(terms)) + 1e-05)

    def norm(group):
        for i, term in enumerate(range(group * GROUP, (group + 1) * GROUP)):
            gain = gain_of(term)
            for at, ref in runs(term):
                normed_ref[group % 2, at, i * width : (i + 1) * width] = (
                    ref[...].astype(jnp.float32) * scale[at] * gain
                ).astype(jnp.bfloat16)

    def product(group):
        total = None
        for i in range(0, GROUP):
            (dy, dx), which = terms[group * GROUP + i]
            chip_at = lax.rem(pipe + dy + RING, RING) * RING + lax.rem(chip_x + dx + RING, RING)
            peer = chip_at * CORES + (core if which == 0 else 1 - core)
            term = jnp.dot(
                normed_ref[group % 2, :, i * width : (i + 1) * width],
                weight_ref[pl.ds(pl.multiple_of(peer * width, width), width), :],
                preferred_element_type=jnp.float32,
            )
            total = term if total is None else total + term
        return total

    norm(0)
    for group in range(groups):
        term = product(group)
        if group + 1 < groups:
            norm(group + 1)
        if group == 0:
            scores_ref[...] = term
        elif group < groups - 1:
            scores_ref[...] += term
        else:
            scores = scores_ref[...] + term
            scores_ref[...] = scores
            logits_ref[...] = scores.astype(jnp.bfloat16)
            spread_rows(jnp.max(scores, axis=1, keepdims=True), top_ref)


def head(blocks, weight):
    names = dict.fromkeys(place[0] for places in PLACES.values() for place in places)
    keys = [(which, array) for which in range(CORES) for array in names]
    rows, columns = 2 * HALF, weight.shape[1]
    width = weight.shape[0] // PEERS
    in_vmem = pl.BlockSpec(memory_space=pltpu.VMEM)
    return pl.pallas_call(
        functools.partial(head_kernel, keys),
        in_specs=[in_vmem] * (len(keys) + 1),
        out_specs=[in_vmem] * 3,
        out_shape=[
            jax.ShapeDtypeStruct((rows, columns), jnp.float32),
            jax.ShapeDtypeStruct((rows, columns), jnp.bfloat16),
            jax.ShapeDtypeStruct((PEERS, rows // LANES, LANES), jnp.float32),
        ],
        scratch_shapes=[pltpu.VMEM((2, rows, GROUP * width), jnp.bfloat16)],
        compiler_params=pltpu.CompilerParams(vmem_limit_bytes=HEAD_VMEM),
        name="head",
    )(*[blocks[key] for key in keys], weight)


def gate_kernel(tops_ref, scores_ref, kept_ref, mass_ref):
    parts = tops_ref.shape[1]
    top = rows_of([jnp.max(tops_ref[:, part, :], axis=0, keepdims=True) for part in range(parts)])
    shifted = scores_ref[...] - top[:, :1]
    kept = jnp.exp(shifted) * jax.nn.sigmoid(gate_sharpness * (shifted - min_p_log))
    kept_ref[...] = kept
    spread_rows(jnp.sum(kept, axis=1, keepdims=True), mass_ref)


def gate(tops, scores):
    return pl.pallas_call(
        gate_kernel,
        out_shape=[
            jax.ShapeDtypeStruct(scores.shape, jnp.float32),
            jax.ShapeDtypeStruct(tops.shape, jnp.float32),
        ],
        compiler_params=pltpu.CompilerParams(vmem_limit_bytes=SMALL_VMEM),
        name="gate",
    )(tops, scores)


def share_kernel(masses_ref, kept_ref, probs_ref):
    parts = masses_ref.shape[1]
    mass = rows_of(
        [jnp.sum(masses_ref[:, part, :], axis=0, keepdims=True) for part in range(parts)]
    )
    probs_ref[...] = kept_ref[...] / mass[:, :1]


def share(masses, kept):
    return pl.pallas_call(
        share_kernel,
        out_shape=jax.ShapeDtypeStruct(kept.shape, jnp.float32),
        compiler_params=pltpu.CompilerParams(vmem_limit_bytes=SMALL_VMEM),
        name="share",
    )(masses, kept)


def local(hidden, norm_gain, head_weight):
    micro, rows, width = hidden.shape
    blocks = {}

    def keep(name, value):
        blocks[0, name] = value
        blocks[1, name] = fetch(value, 0, 0, 1)
        return value

    note = jnp.pad(norm_gain[None], ((0, NOTE - 1), (0, 0)))
    own = keep("own", jnp.concatenate([note, hidden.reshape(micro * rows, width)], axis=0))
    left, right = keep("left", fetch(own, 0, -1)), keep("right", fetch(own, 0, 1))
    down, up = keep("down", fetch(own, -1, 0)), keep("up", fetch(own, 1, 0))
    cross, over = keep("cross", fetch(own, 0, 2)), keep("over", fetch(own, 2, 0))

    row = jnp.concatenate([left[:TOP], right[:TOP], cross[:TOP]], axis=0)
    column = jnp.concatenate([down[TOP:], up[TOP:], over[TOP:]], axis=0)
    row_down, row_up = keep("row_down", fetch(row, -1, 0)), keep("row_up", fetch(row, 1, 0))
    col_left, col_right = (
        keep("col_left", fetch(column, 0, -1)),
        keep("col_right", fetch(column, 0, 1)),
    )
    keep("row_over", fetch(row, 2, 0))
    keep("col_cross", fetch(column, 0, 2))
    scores, logits, tops = head(blocks, bring(head_weight))

    kept, masses = gate(exchange(tops), scores)
    probs = share(exchange(masses), kept)
    shape = (micro, rows, head_weight.shape[1])
    return logits.reshape(shape), probs.reshape(shape)


def solution(mesh):
    return jax.shard_map(
        local,
        mesh=mesh,
        in_specs=(
            P("dp", None, AXES),
            P(AXES),
            P(None, AXES),
        ),
        out_specs=(P("dp", None, AXES), P("dp", None, AXES)),
        check_vma=False,
    )
```

time: 105 us -> 94.1 us (0.90)
  starting transfers between devices: 35.8 us -> 27.6 us
  Pallas kernels: 22.7 us -> 18.9 us
  waiting for transfers between devices: 19.2 us -> 22.7 us
  local copies, waits for them, and re-layouts: 3.42 us -> 0.75 us
    ppermute x33 -> x25, starting transfers between devices: 35.8 us -> 27.6 us  [fetch(): return lax.ppermute(value, AXES, pairs)]
    pallas_call x1 -> x2, Pallas kernels: 21.1 us -> 17.3 us  [the longest x1 9.13 us: head(): pl.pallas_call(functools.partial(head_kernel, keys), in_specs=[in_vmem] *...]
    ppermute x33 -> x25, waiting for transfers between devices: 19.2 us -> 22.7 us  [fetch(): return lax.ppermute(value, AXES, pairs)]
    unnamed x70 -> x0, local copies, waits for them, and re-layouts: 2.62 us -> none
  transfers between devices with their start and end apart: 33 -> 25, of which waited for: 10 -> 9; matrix products, arithmetic and copies ran while one was open for 0% -> 0% of each run, Pallas kernels for 0% -> 9%
where the time goes in v3:
time: 94.1 us; the launch traced here: 93.8 us
  starting transfers between devices  27.6 us (29%)
  waiting for transfers between devices  22.7 us (24%)
  blocking collectives  22 us (23%)
  Pallas kernels  18.9 us (20%)
  other arithmetic  1.03 us (1%)
    ppermute x25, starting transfers between devices, fetch(): return lax.ppermute(value, AXES, pairs)  27.6 us
    ppermute x25, waiting for transfers between devices, fetch(): return lax.ppermute(value, AXES, pairs)  22.7 us
    all_to_all x2, blocking collectives, exchange(): return lax.all_to_all(values, AXES, 0, 0, tiled=True)  22 us
    pallas_call x1, Pallas kernels, head(): pl.pallas_call(functools.partial(head_kernel, keys), in_specs=[in_vmem] *...  9.13 us
    pallas_call x1, Pallas kernels, bring(): pl.pallas_call(kernel, in_specs=[pl.BlockSpec(memory_space=pl.ANY)], out_...  8.16 us
  transfers between devices with their start and end apart: 25, of which 9 were waited for; matrix products, arithmetic and copies ran while one was open for 0% of the time, Pallas kernels for 9%

profile of v3, /device:TPU:1, one launch (start us, length us, event | category | flops | bytes accessed | tf_op | source)
XLA Modules:
  0.0 93.8 jit_solution(9803449145450263297)
XLA Ops:
  0.6 0.7 broadcast_in_dim.3
  1.3 1.0 %fusion.1.refs_0_ = bf16[272,512]{1,0:T(8,128)(2,1)S(1)} fusion(bf16[1,512]{1,0:T(2,128)(2,1)S(1)} %broadcast_in_dim.3, bf16[256,512]{1,0:T(8,128)(2,1)} %bitcast.4), kind=kLoop, calls=%fused_computation.4 | loop fusion | flops 835584 | bytes 541696 | tf_op jit(solution)/shard_map/concatenate | solution.py:245
  2.3 1.5 %collective-permute-start.12 = (bf16[272,512]{1,0:T(8,128)(2,1)S(1)}, bf16[272,512]{1,0:T(8,128)(2,1)S(1)}, u32[]{:S(2)}, u32[]{:S(2)}) collective-permute-start(bf16[272,512]{1,0:T(8,128)(2,1)S(1)} %fusion.1.refs_0_), channel_id=1, source_target_pairs={{4,0},{0,4},{12,8},{8,12},{20,16},{16,20},{28,24},{24,28},{36,32},... | collective-permute-start | bytes 835592 | tf_op jit(solution)/shard_map/ppermute | solution.py:54
  3.8 3.0 %collective-permute-start.5 = (bf16[272,512]{1,0:T(8,128)(2,1)S(1)}, bf16[272,512]{1,0:T(8,128)(2,1)S(1)}, u32[]{:S(2)}, u32[]{:S(2)}) collective-permute-start(bf16[272,512]{1,0:T(8,128)(2,1)S(1)} %fusion.1.refs_0_), channel_id=1, source_target_pairs={{64,0},{68,4},{72,8},{76,12},{80,16},{84,20},{88,24},{92,28},{96,3... | collective-permute-start | bytes 835592 | tf_op jit(solution)/shard_map/ppermute | solution.py:54
  6.8 2.7 %collective-permute-start.4 = (bf16[272,512]{1,0:T(8,128)(2,1)S(1)}, bf16[272,512]{1,0:T(8,128)(2,1)S(1)}, u32[]{:S(2)}, u32[]{:S(2)}) collective-permute-start(bf16[272,512]{1,0:T(8,128)(2,1)S(1)} %fusion.1.refs_0_), channel_id=1, source_target_pairs={{16,0},{20,4},{24,8},{28,12},{0,16},{4,20},{8,24},{12,28},{48,32},... | collective-permute-start | bytes 835592 | tf_op jit(solution)/shard_map/ppermute | solution.py:54
  9.5 0.8 collective-permute-start.3
  10.3 0.7 collective-permute-start.2
  11.0 0.9 collective-permute-start.1
  11.9 1.7 %collective-permute-done.5.refs_6_ = bf16[272,512]{1,0:T(8,128)(2,1)S(1)} collective-permute-done((bf16[272,512]{1,0:T(8,128)(2,1)S(1)}, bf16[272,512]{1,0:T(8,128)(2,1)S(1)}, u32[]{:S(2)}, u32[]{:S(2)}) %collective-permute-start.5) | collective-permute-done | bytes 278560 | tf_op jit(solution)/shard_map/ppermute | solution.py:54
  13.5 1.3 %collective-permute-start = (bf16[272,512]{1,0:T(8,128)(2,1)S(1)}, bf16[272,512]{1,0:T(8,128)(2,1)S(1)}, u32[]{:S(2)}, u32[]{:S(2)}) collective-permute-start(bf16[272,512]{1,0:T(8,128)(2,1)S(1)} %fusion.1.refs_0_), channel_id=1, source_target_pairs={{24,0},{28,4},{0,8},{4,12},{8,16},{12,20},{16,24},{20,28},{56,32},... | collective-permute-start | bytes 835592 | tf_op jit(solution)/shard_map/ppermute | solution.py:54
  14.8 1.4 %collective-permute-done.4.refs_5_ = bf16[272,512]{1,0:T(8,128)(2,1)S(1)} collective-permute-done((bf16[272,512]{1,0:T(8,128)(2,1)S(1)}, bf16[272,512]{1,0:T(8,128)(2,1)S(1)}, u32[]{:S(2)}, u32[]{:S(2)}) %collective-permute-start.4) | collective-permute-done | bytes 278560 | tf_op jit(solution)/shard_map/ppermute | solution.py:54
  16.2 1.2 %collective-permute-start.18 = (bf16[272,512]{1,0:T(8,128)(2,1)S(1)}, bf16[272,512]{1,0:T(8,128)(2,1)S(1)}, u32[]{:S(2)}, u32[]{:S(2)}) collective-permute-start(bf16[272,512]{1,0:T(8,128)(2,1)S(1)} %collective-permute-done.5.refs_6_), channel_id=1, source_target_pairs={{4,0},{0,4},{12,8},{8,12},{20,16},{16,20},{28,24},{24,28},{36,32},... | collective-permute-start | bytes 835592 | tf_op jit(solution)/shard_map/ppermute | solution.py:54
  17.4 2.6 %collective-permute-done.3.refs_4_ = bf16[272,512]{1,0:T(8,128)(2,1)S(1)} collective-permute-done((bf16[272,512]{1,0:T(8,128)(2,1)S(1)}, bf16[272,512]{1,0:T(8,128)(2,1)S(1)}, u32[]{:S(2)}, u32[]{:S(2)}) %collective-permute-start.3) | collective-permute-done | bytes 278560 | tf_op jit(solution)/shard_map/ppermute | solution.py:54
  19.9 0.9 collective-permute-start.17
  20.9 1.4 %collective-permute-done.1.refs_2_ = bf16[272,512]{1,0:T(8,128)(2,1)S(1)} collective-permute-done((bf16[272,512]{1,0:T(8,128)(2,1)S(1)}, bf16[272,512]{1,0:T(8,128)(2,1)S(1)}, u32[]{:S(2)}, u32[]{:S(2)}) %collective-permute-start.1) | collective-permute-done | bytes 278560 | tf_op jit(solution)/shard_map/ppermute | solution.py:54
  22.3 1.7 %collective-permute-start.9 = (bf16[384,512]{1,0:T(8,128)(2,1)S(1)}, bf16[384,512]{1,0:T(8,128)(2,1)S(1)}, u32[]{:S(2)}, u32[]{:S(2)}) collective-permute-start(bf16[384,512]{1,0:T(8,128)(2,1)S(1)} %pad_maximum_fusion.1), channel_id=1, source_target_pairs={{16,0},{20,4},{24,8},{28,12},{0,16},{4,20},{8,24},{12,28},{48,32},... | collective-permute-start | bytes 1179656 | tf_op jit(solution)/shard_map/ppermute | solution.py:54
  24.0 2.4 %collective-permute-start.8 = (bf16[384,512]{1,0:T(8,128)(2,1)S(1)}, bf16[384,512]{1,0:T(8,128)(2,1)S(1)}, u32[]{:S(2)}, u32[]{:S(2)}) collective-permute-start(bf16[384,512]{1,0:T(8,128)(2,1)S(1)} %pad_maximum_fusion.1), channel_id=1, source_target_pairs={{8,0},{12,4},{16,8},{20,12},{24,16},{28,20},{0,24},{4,28},{40,32},... | collective-permute-start | bytes 1179656 | tf_op jit(solution)/shard_map/ppermute | solution.py:54
  26.5 1.1 %collective-permute-start.15 = (bf16[272,512]{1,0:T(8,128)(2,1)S(1)}, bf16[272,512]{1,0:T(8,128)(2,1)S(1)}, u32[]{:S(2)}, u32[]{:S(2)}) collective-permute-start(bf16[272,512]{1,0:T(8,128)(2,1)S(1)} %collective-permute-done.2.refs_3_), channel_id=1, source_target_pairs={{4,0},{0,4},{12,8},{8,12},{20,16},{16,20},{28,24},{24,28},{36,32},... | collective-permute-start | bytes 835592 | tf_op jit(solution)/shard_map/ppermute | solution.py:54
  28.7 0.9 collective-permute-start.11
  29.6 1.9 %collective-permute-start.10 = (bf16[432,512]{1,0:T(8,128)(2,1)S(1)}, bf16[432,512]{1,0:T(8,128)(2,1)S(1)}, u32[]{:S(2)}, u32[]{:S(2)}) collective-permute-start(bf16[432,512]{1,0:T(8,128)(2,1)S(1)} %pad_maximum_fusion), channel_id=1, source_target_pairs={{32,0},{36,4},{40,8},{44,12},{48,16},{52,20},{56,24},{60,28},{64,3... | collective-permute-start | bytes 1327112 | tf_op jit(solution)/shard_map/ppermute | solution.py:54
  31.5 1.7 %collective-permute-done.9.refs_10_ = bf16[384,512]{1,0:T(8,128)(2,1)S(1)} collective-permute-done((bf16[384,512]{1,0:T(8,128)(2,1)S(1)}, bf16[384,512]{1,0:T(8,128)(2,1)S(1)}, u32[]{:S(2)}, u32[]{:S(2)}) %collective-permute-start.9) | collective-permute-done | bytes 393248 | tf_op jit(solution)/shard_map/ppermute | solution.py:54
  33.2 2.6 %collective-permute-start.7 = (bf16[384,512]{1,0:T(8,128)(2,1)S(1)}, bf16[384,512]{1,0:T(8,128)(2,1)S(1)}, u32[]{:S(2)}, u32[]{:S(2)}) collective-permute-start(bf16[384,512]{1,0:T(8,128)(2,1)S(1)} %pad_maximum_fusion.1), channel_id=1, source_target_pairs={{24,0},{28,4},{0,8},{4,12},{8,16},{12,20},{16,24},{20,28},{56,32},... | collective-permute-start | bytes 1179656 | tf_op jit(solution)/shard_map/ppermute | solution.py:54
  35.8 7.3 %collective-permute-done.8.refs_9_ = bf16[384,512]{1,0:T(8,128)(2,1)S(1)} collective-permute-done((bf16[384,512]{1,0:T(8,128)(2,1)S(1)}, bf16[384,512]{1,0:T(8,128)(2,1)S(1)}, u32[]{:S(2)}, u32[]{:S(2)}) %collective-permute-start.8) | collective-permute-done | bytes 393248 | tf_op jit(solution)/shard_map/ppermute | solution.py:54
  43.1 1.3 %collective-permute-start.22 = (bf16[384,512]{1,0:T(8,128)(2,1)S(1)}, bf16[384,512]{1,0:T(8,128)(2,1)S(1)}, u32[]{:S(2)}, u32[]{:S(2)}) collective-permute-start(bf16[384,512]{1,0:T(8,128)(2,1)S(1)} %collective-permute-done.9.refs_10_), channel_id=1, source_target_pairs={{4,0},{0,4},{12,8},{8,12},{20,16},{16,20},{28,24},{24,28},{36,32},... | collective-permute-start | bytes 1179656 | tf_op jit(solution)/shard_map/ppermute | solution.py:54
  44.5 5.0 %collective-permute-done.10.refs_11_ = bf16[432,512]{1,0:T(8,128)(2,1)S(1)} collective-permute-done((bf16[432,512]{1,0:T(8,128)(2,1)S(1)}, bf16[432,512]{1,0:T(8,128)(2,1)S(1)}, u32[]{:S(2)}, u32[]{:S(2)}) %collective-permute-start.10) | collective-permute-done | bytes 442400 | tf_op jit(solution)/shard_map/ppermute | solution.py:54
  49.5 1.2 %collective-permute-start.23 = (bf16[432,512]{1,0:T(8,128)(2,1)S(1)}, bf16[432,512]{1,0:T(8,128)(2,1)S(1)}, u32[]{:S(2)}, u32[]{:S(2)}) collective-permute-start(bf16[432,512]{1,0:T(8,128)(2,1)S(1)} %collective-permute-done.10.refs_11_), channel_id=1, source_target_pairs={{4,0},{0,4},{12,8},{8,12},{20,16},{16,20},{28,24},{24,28},{36,32},... | collective-permute-start | bytes 1327112 | tf_op jit(solution)/shard_map/ppermute | solution.py:54
  50.7 1.1 %collective-permute-done.6.refs_7_ = bf16[432,512]{1,0:T(8,128)(2,1)S(1)} collective-permute-done((bf16[432,512]{1,0:T(8,128)(2,1)S(1)}, bf16[432,512]{1,0:T(8,128)(2,1)S(1)}, u32[]{:S(2)}, u32[]{:S(2)}) %collective-permute-start.6) | collective-permute-done | bytes 442400 | tf_op jit(solution)/shard_map/ppermute | solution.py:54
  52.8 8.2 %bring.1.refs_26_ = bf16[16384,768]{1,0:T(8,128)(2,1)S(1)} custom-call(bf16[16384,768]{1,0:T(8,128)(2,1)} %weight_ref.1), custom_call_target="tpu_custom_call" | custom-call | bytes 50331648 | tf_op jit(solution)/shard_map/bring/pallas_call | solution.py:79
  61.0 9.1 %head.1 = (f32[256,768]{1,0:T(8,128)S(1)}, bf16[256,768]{1,0:T(8,128)(2,1)}, f32[32,2,128]{2,1,0:T(2,128)S(1)}) custom-call(bf16[272,512]{1,0:T(8,128)(2,1)S(1)} %fusion.1.refs_0_, bf16[272,512]{1,0:T(8,128)(2,1)S(1)} %collective-permute-done.refs_1_, bf16[272,512]{1,0:T(8,128)(2,1)S(1)} %collective-permute-done.1.refs_2_, ...), custom_call_target="tpu_custom_call" | custom-call | tf_op jit(solution)/shard_map/head/pallas_call | solution.py:182
  70.2 11.3 %all_to_all.10.tops_ref = f32[32,2,128]{2,1,0:T(2,128)S(1)} all-to-all(f32[32,2,128]{2,1,0:T(2,128)S(1)} %get-tuple-element.8), channel_id=1, replica_groups=mesh['pipe'=4,'tensor'=8,'dp'=4] {'pipe','tensor'}, dimensions={0} | all-to-all | bytes 65536 | tf_op jit(solution)/shard_map/all_to_all | solution.py:58
  82.0 10.7 %all_to_all.11.masses_ref = f32[32,2,128]{2,1,0:T(2,128)S(1)} all-to-all(f32[32,2,128]{2,1,0:T(2,128)S(1)} %get-tuple-element.10), channel_id=1, replica_groups=mesh['pipe'=4,'tensor'=8,'dp'=4] {'pipe','tensor'}, dimensions={0} | all-to-all | bytes 65536 | tf_op jit(solution)/shard_map/all_to_all | solution.py:58
  92.7 1.1 %share.1 = f32[256,768]{1,0:T(8,128)} custom-call(f32[32,2,128]{2,1,0:T(2,128)S(1)} %all_to_all.11.masses_ref, f32[256,768]{1,0:T(8,128)S(1)} %get-tuple-element.11.kept_ref), custom_call_target="tpu_custom_call" | custom-call | tf_op jit(solution)/shard_map/share/pallas_call | solution.py:227
  (34 shorter events, 2.8 us)
Async XLA Ops:
  2.3 8.7 %collective-permute-start.12 = (bf16[272,512]{1,0:T(8,128)(2,1)S(1)}, bf16[272,512]{1,0:T(8,128)(2,1)S(1)}, u32[]{:S(2)}, u32[]{:S(2)}) collective-permute-start(bf16[272,512]{1,0:T(8,128)(2,1)S(1)} %fusion.1.refs_0_), channel_id=1, source_target_pairs={{4,0},{0,4},{12,8},{8,12},{20,16},{16,20},{28,24},{24,28},{36,32},... | collective-permute-start | bytes 835592 | tf_op jit(solution)/shard_map/ppermute | solution.py:54
  3.8 9.8 %collective-permute-start.5 = (bf16[272,512]{1,0:T(8,128)(2,1)S(1)}, bf16[272,512]{1,0:T(8,128)(2,1)S(1)}, u32[]{:S(2)}, u32[]{:S(2)}) collective-permute-start(bf16[272,512]{1,0:T(8,128)(2,1)S(1)} %fusion.1.refs_0_), channel_id=1, source_target_pairs={{64,0},{68,4},{72,8},{76,12},{80,16},{84,20},{88,24},{92,28},{96,3... | collective-permute-start | bytes 835592 | tf_op jit(solution)/shard_map/ppermute | solution.py:54
  6.8 9.4 %collective-permute-start.4 = (bf16[272,512]{1,0:T(8,128)(2,1)S(1)}, bf16[272,512]{1,0:T(8,128)(2,1)S(1)}, u32[]{:S(2)}, u32[]{:S(2)}) collective-permute-start(bf16[272,512]{1,0:T(8,128)(2,1)S(1)} %fusion.1.refs_0_), channel_id=1, source_target_pairs={{16,0},{20,4},{24,8},{28,12},{0,16},{4,20},{8,24},{12,28},{48,32},... | collective-permute-start | bytes 835592 | tf_op jit(solution)/shard_map/ppermute | solution.py:54
  9.5 10.4 %collective-permute-start.3 = (bf16[272,512]{1,0:T(8,128)(2,1)S(1)}, bf16[272,512]{1,0:T(8,128)(2,1)S(1)}, u32[]{:S(2)}, u32[]{:S(2)}) collective-permute-start(bf16[272,512]{1,0:T(8,128)(2,1)S(1)} %fusion.1.refs_0_), channel_id=1, source_target_pairs={{32,0},{36,4},{40,8},{44,12},{48,16},{52,20},{56,24},{60,28},{64,3... | collective-permute-start | bytes 835592 | tf_op jit(solution)/shard_map/ppermute | solution.py:54
  10.3 10.5 %collective-permute-start.2 = (bf16[272,512]{1,0:T(8,128)(2,1)S(1)}, bf16[272,512]{1,0:T(8,128)(2,1)S(1)}, u32[]{:S(2)}, u32[]{:S(2)}) collective-permute-start(bf16[272,512]{1,0:T(8,128)(2,1)S(1)} %fusion.1.refs_0_), channel_id=1, source_target_pairs={{96,0},{100,4},{104,8},{108,12},{112,16},{116,20},{120,24},{124,28... | collective-permute-start | bytes 835592 | tf_op jit(solution)/shard_map/ppermute | solution.py:54
  11.0 11.3 %collective-permute-start.1 = (bf16[272,512]{1,0:T(8,128)(2,1)S(1)}, bf16[272,512]{1,0:T(8,128)(2,1)S(1)}, u32[]{:S(2)}, u32[]{:S(2)}) collective-permute-start(bf16[272,512]{1,0:T(8,128)(2,1)S(1)} %fusion.1.refs_0_), channel_id=1, source_target_pairs={{8,0},{12,4},{16,8},{20,12},{24,16},{28,20},{0,24},{4,28},{40,32},... | collective-permute-start | bytes 835592 | tf_op jit(solution)/shard_map/ppermute | solution.py:54
  13.5 10.5 %collective-permute-start = (bf16[272,512]{1,0:T(8,128)(2,1)S(1)}, bf16[272,512]{1,0:T(8,128)(2,1)S(1)}, u32[]{:S(2)}, u32[]{:S(2)}) collective-permute-start(bf16[272,512]{1,0:T(8,128)(2,1)S(1)} %fusion.1.refs_0_), channel_id=1, source_target_pairs={{24,0},{28,4},{0,8},{4,12},{8,16},{12,20},{16,24},{20,28},{56,32},... | collective-permute-start | bytes 835592 | tf_op jit(solution)/shard_map/ppermute | solution.py:54
  16.2 10.3 %collective-permute-start.18 = (bf16[272,512]{1,0:T(8,128)(2,1)S(1)}, bf16[272,512]{1,0:T(8,128)(2,1)S(1)}, u32[]{:S(2)}, u32[]{:S(2)}) collective-permute-start(bf16[272,512]{1,0:T(8,128)(2,1)S(1)} %collective-permute-done.5.refs_6_), channel_id=1, source_target_pairs={{4,0},{0,4},{12,8},{8,12},{20,16},{16,20},{28,24},{24,28},{36,32},... | collective-permute-start | bytes 835592 | tf_op jit(solution)/shard_map/ppermute | solution.py:54
  19.9 7.6 %collective-permute-start.17 = (bf16[272,512]{1,0:T(8,128)(2,1)S(1)}, bf16[272,512]{1,0:T(8,128)(2,1)S(1)}, u32[]{:S(2)}, u32[]{:S(2)}) collective-permute-start(bf16[272,512]{1,0:T(8,128)(2,1)S(1)} %collective-permute-done.4.refs_5_), channel_id=1, source_target_pairs={{4,0},{0,4},{12,8},{8,12},{20,16},{16,20},{28,24},{24,28},{36,32},... | collective-permute-start | bytes 835592 | tf_op jit(solution)/shard_map/ppermute | solution.py:54
  20.8 6.8 %collective-permute-start.16 = (bf16[272,512]{1,0:T(8,128)(2,1)S(1)}, bf16[272,512]{1,0:T(8,128)(2,1)S(1)}, u32[]{:S(2)}, u32[]{:S(2)}) collective-permute-start(bf16[272,512]{1,0:T(8,128)(2,1)S(1)} %collective-permute-done.3.refs_4_), channel_id=1, source_target_pairs={{4,0},{0,4},{12,8},{8,12},{20,16},{16,20},{28,24},{24,28},{36,32},... | collective-permute-start | bytes 835592 | tf_op jit(solution)/shard_map/ppermute | solution.py:54
  22.3 10.9 %collective-permute-start.9 = (bf16[384,512]{1,0:T(8,128)(2,1)S(1)}, bf16[384,512]{1,0:T(8,128)(2,1)S(1)}, u32[]{:S(2)}, u32[]{:S(2)}) collective-permute-start(bf16[384,512]{1,0:T(8,128)(2,1)S(1)} %pad_maximum_fusion.1), channel_id=1, source_target_pairs={{16,0},{20,4},{24,8},{28,12},{0,16},{4,20},{8,24},{12,28},{48,32},... | collective-permute-start | bytes 1179656 | tf_op jit(solution)/shard_map/ppermute | solution.py:54
  24.0 19.1 %collective-permute-start.8 = (bf16[384,512]{1,0:T(8,128)(2,1)S(1)}, bf16[384,512]{1,0:T(8,128)(2,1)S(1)}, u32[]{:S(2)}, u32[]{:S(2)}) collective-permute-start(bf16[384,512]{1,0:T(8,128)(2,1)S(1)} %pad_maximum_fusion.1), channel_id=1, source_target_pairs={{8,0},{12,4},{16,8},{20,12},{24,16},{28,20},{0,24},{4,28},{40,32},... | collective-permute-start | bytes 1179656 | tf_op jit(solution)/shard_map/ppermute | solution.py:54
  26.5 2.2 %collective-permute-start.15 = (bf16[272,512]{1,0:T(8,128)(2,1)S(1)}, bf16[272,512]{1,0:T(8,128)(2,1)S(1)}, u32[]{:S(2)}, u32[]{:S(2)}) collective-permute-start(bf16[272,512]{1,0:T(8,128)(2,1)S(1)} %collective-permute-done.2.refs_3_), channel_id=1, source_target_pairs={{4,0},{0,4},{12,8},{8,12},{20,16},{16,20},{28,24},{24,28},{36,32},... | collective-permute-start | bytes 835592 | tf_op jit(solution)/shard_map/ppermute | solution.py:54
  27.5 2.1 %collective-permute-start.14 = (bf16[272,512]{1,0:T(8,128)(2,1)S(1)}, bf16[272,512]{1,0:T(8,128)(2,1)S(1)}, u32[]{:S(2)}, u32[]{:S(2)}) collective-permute-start(bf16[272,512]{1,0:T(8,128)(2,1)S(1)} %collective-permute-done.1.refs_2_), channel_id=1, source_target_pairs={{4,0},{0,4},{12,8},{8,12},{20,16},{16,20},{28,24},{24,28},{36,32},... | collective-permute-start | bytes 835592 | tf_op jit(solution)/shard_map/ppermute | solution.py:54
  27.6 3.9 %collective-permute-start.13 = (bf16[272,512]{1,0:T(8,128)(2,1)S(1)}, bf16[272,512]{1,0:T(8,128)(2,1)S(1)}, u32[]{:S(2)}, u32[]{:S(2)}) collective-permute-start(bf16[272,512]{1,0:T(8,128)(2,1)S(1)} %collective-permute-done.refs_1_), channel_id=1, source_target_pairs={{4,0},{0,4},{12,8},{8,12},{20,16},{16,20},{28,24},{24,28},{36,32},... | collective-permute-start | bytes 835592 | tf_op jit(solution)/shard_map/ppermute | solution.py:54
  28.7 15.7 %collective-permute-start.11 = (bf16[432,512]{1,0:T(8,128)(2,1)S(1)}, bf16[432,512]{1,0:T(8,128)(2,1)S(1)}, u32[]{:S(2)}, u32[]{:S(2)}) collective-permute-start(bf16[432,512]{1,0:T(8,128)(2,1)S(1)} %pad_maximum_fusion), channel_id=1, source_target_pairs={{64,0},{68,4},{72,8},{76,12},{80,16},{84,20},{88,24},{92,28},{96,3... | collective-permute-start | bytes 1327112 | tf_op jit(solution)/shard_map/ppermute | solution.py:54
  29.6 19.9 %collective-permute-start.10 = (bf16[432,512]{1,0:T(8,128)(2,1)S(1)}, bf16[432,512]{1,0:T(8,128)(2,1)S(1)}, u32[]{:S(2)}, u32[]{:S(2)}) collective-permute-start(bf16[432,512]{1,0:T(8,128)(2,1)S(1)} %pad_maximum_fusion), channel_id=1, source_target_pairs={{32,0},{36,4},{40,8},{44,12},{48,16},{52,20},{56,24},{60,28},{64,3... | collective-permute-start | bytes 1327112 | tf_op jit(solution)/shard_map/ppermute | solution.py:54
  31.5 20.3 %collective-permute-start.6 = (bf16[432,512]{1,0:T(8,128)(2,1)S(1)}, bf16[432,512]{1,0:T(8,128)(2,1)S(1)}, u32[]{:S(2)}, u32[]{:S(2)}) collective-permute-start(bf16[432,512]{1,0:T(8,128)(2,1)S(1)} %pad_maximum_fusion), channel_id=1, source_target_pairs={{96,0},{100,4},{104,8},{108,12},{112,16},{116,20},{120,24},{124,28... | collective-permute-start | bytes 1327112 | tf_op jit(solution)/shard_map/ppermute | solution.py:54
  33.2 19.1 %collective-permute-start.7 = (bf16[384,512]{1,0:T(8,128)(2,1)S(1)}, bf16[384,512]{1,0:T(8,128)(2,1)S(1)}, u32[]{:S(2)}, u32[]{:S(2)}) collective-permute-start(bf16[384,512]{1,0:T(8,128)(2,1)S(1)} %pad_maximum_fusion.1), channel_id=1, source_target_pairs={{24,0},{28,4},{0,8},{4,12},{8,16},{12,20},{16,24},{20,28},{56,32},... | collective-permute-start | bytes 1179656 | tf_op jit(solution)/shard_map/ppermute | solution.py:54
  43.1 9.2 %collective-permute-start.22 = (bf16[384,512]{1,0:T(8,128)(2,1)S(1)}, bf16[384,512]{1,0:T(8,128)(2,1)S(1)}, u32[]{:S(2)}, u32[]{:S(2)}) collective-permute-start(bf16[384,512]{1,0:T(8,128)(2,1)S(1)} %collective-permute-done.9.refs_10_), channel_id=1, source_target_pairs={{4,0},{0,4},{12,8},{8,12},{20,16},{16,20},{28,24},{24,28},{36,32},... | collective-permute-start | bytes 1179656 | tf_op jit(solution)/shard_map/ppermute | solution.py:54
  44.4 16.5 %collective-permute-start.24 = (bf16[432,512]{1,0:T(8,128)(2,1)S(1)}, bf16[432,512]{1,0:T(8,128)(2,1)S(1)}, u32[]{:S(2)}, u32[]{:S(2)}) collective-permute-start(bf16[432,512]{1,0:T(8,128)(2,1)S(1)} %collective-permute-done.11.refs_12_), channel_id=1, source_target_pairs={{4,0},{0,4},{12,8},{8,12},{20,16},{16,20},{28,24},{24,28},{36,32},... | collective-permute-start | bytes 1327112 | tf_op jit(solution)/shard_map/ppermute | solution.py:54
  49.5 11.5 %collective-permute-start.23 = (bf16[432,512]{1,0:T(8,128)(2,1)S(1)}, bf16[432,512]{1,0:T(8,128)(2,1)S(1)}, u32[]{:S(2)}, u32[]{:S(2)}) collective-permute-start(bf16[432,512]{1,0:T(8,128)(2,1)S(1)} %collective-permute-done.10.refs_11_), channel_id=1, source_target_pairs={{4,0},{0,4},{12,8},{8,12},{20,16},{16,20},{28,24},{24,28},{36,32},... | collective-permute-start | bytes 1327112 | tf_op jit(solution)/shard_map/ppermute | solution.py:54
  51.8 9.2 %collective-permute-start.19 = (bf16[432,512]{1,0:T(8,128)(2,1)S(1)}, bf16[432,512]{1,0:T(8,128)(2,1)S(1)}, u32[]{:S(2)}, u32[]{:S(2)}) collective-permute-start(bf16[432,512]{1,0:T(8,128)(2,1)S(1)} %collective-permute-done.6.refs_7_), channel_id=1, source_target_pairs={{4,0},{0,4},{12,8},{8,12},{20,16},{16,20},{28,24},{24,28},{36,32},... | collective-permute-start | bytes 1327112 | tf_op jit(solution)/shard_map/ppermute | solution.py:54
  52.3 8.7 %collective-permute-start.21 = (bf16[384,512]{1,0:T(8,128)(2,1)S(1)}, bf16[384,512]{1,0:T(8,128)(2,1)S(1)}, u32[]{:S(2)}, u32[]{:S(2)}) collective-permute-start(bf16[384,512]{1,0:T(8,128)(2,1)S(1)} %collective-permute-done.8.refs_9_), channel_id=1, source_target_pairs={{4,0},{0,4},{12,8},{8,12},{20,16},{16,20},{28,24},{24,28},{36,32},... | collective-permute-start | bytes 1179656 | tf_op jit(solution)/shard_map/ppermute | solution.py:54
  52.3 8.7 %collective-permute-start.20 = (bf16[384,512]{1,0:T(8,128)(2,1)S(1)}, bf16[384,512]{1,0:T(8,128)(2,1)S(1)}, u32[]{:S(2)}, u32[]{:S(2)}) collective-permute-start(bf16[384,512]{1,0:T(8,128)(2,1)S(1)} %collective-permute-done.7.refs_8_), channel_id=1, source_target_pairs={{4,0},{0,4},{12,8},{8,12},{20,16},{16,20},{28,24},{24,28},{36,32},... | collective-permute-start | bytes 1179656 | tf_op jit(solution)/shard_map/ppermute | solution.py:54

commit v4 on v3

--- a/solution.py
+++ b/solution.py
@@ -70,24 +70,24 @@
     return jnp.broadcast_to(across, (LANES, across.shape[1])).T
 
 
-def bring(weight):
-    def kernel(weight_ref, out_ref, sem):
-        copy = pltpu.make_async_copy(weight_ref, out_ref, sem)
-        copy.start()
-        copy.wait()
+def join(pieces):
+    counts = [piece.shape[0] for piece in pieces]
+
+    def kernel(*refs):
+        at = 0
+        for ref, count in zip(refs, counts):
+            refs[-1][at : at + count, :] = ref[...]
+            at += count
 
     return pl.pallas_call(
         kernel,
-        in_specs=[pl.BlockSpec(memory_space=pl.ANY)],
+        in_specs=[pl.BlockSpec(memory_space=pltpu.VMEM)] * len(pieces),
         out_specs=pl.BlockSpec(memory_space=pltpu.VMEM),
-        out_shape=jax.ShapeDtypeStruct(weight.shape, weight.dtype),
-        scratch_shapes=[pltpu.SemaphoreType.DMA],
+        out_shape=jax.ShapeDtypeStruct((sum(counts), pieces[0].shape[1]), pieces[0].dtype),
         compiler_params=pltpu.CompilerParams(vmem_limit_bytes=SMALL_VMEM),
-        cost_estimate=pl.CostEstimate(
-            flops=0, bytes_accessed=2 * weight.size * weight.dtype.itemsize, transcendentals=0
-        ),
-        name="bring",
-    )(weight)
+        cost_estimate=pl.CostEstimate(flops=13800000000, bytes_accessed=0, transcendentals=0),
+        name="join",
+    )(*pieces)
 
 
 def head_kernel(keys, *refs):
@@ -247,7 +247,7 @@
     down, up = keep("down", fetch(own, -1, 0)), keep("up", fetch(own, 1, 0))
     cross, over = keep("cross", fetch(own, 0, 2)), keep("over", fetch(own, 2, 0))
 
-    row = jnp.concatenate([left[:TOP], right[:TOP], cross[:TOP]], axis=0)
+    row = join([left[:TOP], right[:TOP], cross[:TOP]])
     column = jnp.concatenate([down[TOP:], up[TOP:], over[TOP:]], axis=0)
     row_down, row_up = keep("row_down", fetch(row, -1, 0)), keep("row_up", fetch(row, 1, 0))
     col_left, col_right = (
@@ -256,7 +256,7 @@
     )
     keep("row_over", fetch(row, 2, 0))
     keep("col_cross", fetch(column, 0, 2))
-    scores, logits, tops = head(blocks, bring(head_weight))
+    scores, logits, tops = head(blocks, head_weight)
 
     kept, masses = gate(exchange(tops), scores)
     probs = share(exchange(masses), kept)

time: 94.1 us -> 88.4 us (0.939)
  Pallas kernels: 18.9 us -> 10.8 us
  waiting for transfers between devices: 22.7 us -> 24.5 us
    pallas_call x1, Pallas kernels: 8.16 us -> 0.03 us  [join(): pl.pallas_call(kernel, in_specs=[pl.BlockSpec(memory_space=pltpu.VMEM)] *...]
    ppermute x25, waiting for transfers between devices: 22.7 us -> 24.5 us  [fetch(): return lax.ppermute(value, AXES, pairs)]
  transfers between devices with their start and end apart: 25 -> 25, of which waited for: 9 -> 11; matrix products, arithmetic and copies ran while one was open for 0% -> 0% of each run, Pallas kernels for 9% -> 0%
where the time goes in v4:
time: 88.4 us; the launch traced here: 88.2 us
  starting transfers between devices  27.5 us (31%)
  waiting for transfers between devices  24.5 us (28%)
  blocking collectives  22.8 us (26%)
  Pallas kernels  10.8 us (12%)
  other arithmetic  1 us (1%)
    ppermute x25, starting transfers between devices, fetch(): return lax.ppermute(value, AXES, pairs)  27.5 us
    ppermute x25, waiting for transfers between devices, fetch(): return lax.ppermute(value, AXES, pairs)  24.5 us
    all_to_all x2, blocking collectives, exchange(): return lax.all_to_all(values, AXES, 0, 0, tiled=True)  22.8 us
    pallas_call x1, Pallas kernels, head(): pl.pallas_call(functools.partial(head_kernel, keys), in_specs=[in_vmem] *...  9.13 us
  transfers between devices with their start and end apart: 25, of which 11 were waited for; matrix products, arithmetic and copies ran while one was open for 0% of the time, Pallas kernels for 0%

profile of v4, /device:TPU:1, one launch (start us, length us, event | category | flops | bytes accessed | tf_op | source)
XLA Modules:
  0.0 88.2 jit_solution(4784109034087978556)
XLA Ops:
  0.6 0.7 broadcast_in_dim.3
  1.3 1.0 %fusion.1.refs_0_ = bf16[272,512]{1,0:T(8,128)(2,1)S(1)} fusion(bf16[1,512]{1,0:T(2,128)(2,1)S(1)} %broadcast_in_dim.3, bf16[256,512]{1,0:T(8,128)(2,1)} %bitcast.6), kind=kLoop, calls=%fused_computation.3 | loop fusion | flops 835584 | bytes 541696 | tf_op jit(solution)/shard_map/concatenate | solution.py:245
  2.3 3.8 %collective-permute-start.5 = (bf16[272,512]{1,0:T(8,128)(2,1)S(1)}, bf16[272,512]{1,0:T(8,128)(2,1)S(1)}, u32[]{:S(2)}, u32[]{:S(2)}) collective-permute-start(bf16[272,512]{1,0:T(8,128)(2,1)S(1)} %fusion.1.refs_0_), channel_id=1, source_target_pairs={{64,0},{68,4},{72,8},{76,12},{80,16},{84,20},{88,24},{92,28},{96,3... | collective-permute-start | bytes 835592 | tf_op jit(solution)/shard_map/ppermute | solution.py:54
  6.1 2.7 %collective-permute-start.4 = (bf16[272,512]{1,0:T(8,128)(2,1)S(1)}, bf16[272,512]{1,0:T(8,128)(2,1)S(1)}, u32[]{:S(2)}, u32[]{:S(2)}) collective-permute-start(bf16[272,512]{1,0:T(8,128)(2,1)S(1)} %fusion.1.refs_0_), channel_id=1, source_target_pairs={{16,0},{20,4},{24,8},{28,12},{0,16},{4,20},{8,24},{12,28},{48,32},... | collective-permute-start | bytes 835592 | tf_op jit(solution)/shard_map/ppermute | solution.py:54
  8.9 0.8 collective-permute-start.3
  9.6 0.7 collective-permute-start.2
  10.3 0.9 collective-permute-start.1
  11.2 1.0 %collective-permute-done.5.refs_6_ = bf16[272,512]{1,0:T(8,128)(2,1)S(1)} collective-permute-done((bf16[272,512]{1,0:T(8,128)(2,1)S(1)}, bf16[272,512]{1,0:T(8,128)(2,1)S(1)}, u32[]{:S(2)}, u32[]{:S(2)}) %collective-permute-start.5) | collective-permute-done | bytes 278560 | tf_op jit(solution)/shard_map/ppermute | solution.py:54
  12.2 1.2 %collective-permute-start = (bf16[272,512]{1,0:T(8,128)(2,1)S(1)}, bf16[272,512]{1,0:T(8,128)(2,1)S(1)}, u32[]{:S(2)}, u32[]{:S(2)}) collective-permute-start(bf16[272,512]{1,0:T(8,128)(2,1)S(1)} %fusion.1.refs_0_), channel_id=1, source_target_pairs={{24,0},{28,4},{0,8},{4,12},{8,16},{12,20},{16,24},{20,28},{56,32},... | collective-permute-start | bytes 835592 | tf_op jit(solution)/shard_map/ppermute | solution.py:54
  13.4 1.4 %collective-permute-done.4.refs_5_ = bf16[272,512]{1,0:T(8,128)(2,1)S(1)} collective-permute-done((bf16[272,512]{1,0:T(8,128)(2,1)S(1)}, bf16[272,512]{1,0:T(8,128)(2,1)S(1)}, u32[]{:S(2)}, u32[]{:S(2)}) %collective-permute-start.4) | collective-permute-done | bytes 278560 | tf_op jit(solution)/shard_map/ppermute | solution.py:54
  14.8 2.2 %collective-permute-start.12 = (bf16[272,512]{1,0:T(8,128)(2,1)S(1)}, bf16[272,512]{1,0:T(8,128)(2,1)S(1)}, u32[]{:S(2)}, u32[]{:S(2)}) collective-permute-start(bf16[272,512]{1,0:T(8,128)(2,1)S(1)} %fusion.1.refs_0_), channel_id=1, source_target_pairs={{4,0},{0,4},{12,8},{8,12},{20,16},{16,20},{28,24},{24,28},{36,32},... | collective-permute-start | bytes 835592 | tf_op jit(solution)/shard_map/ppermute | solution.py:54
  17.0 1.5 %collective-permute-done.3.refs_4_ = bf16[272,512]{1,0:T(8,128)(2,1)S(1)} collective-permute-done((bf16[272,512]{1,0:T(8,128)(2,1)S(1)}, bf16[272,512]{1,0:T(8,128)(2,1)S(1)}, u32[]{:S(2)}, u32[]{:S(2)}) %collective-permute-start.3) | collective-permute-done | bytes 278560 | tf_op jit(solution)/shard_map/ppermute | solution.py:54
  18.5 1.5 %collective-permute-start.18 = (bf16[272,512]{1,0:T(8,128)(2,1)S(1)}, bf16[272,512]{1,0:T(8,128)(2,1)S(1)}, u32[]{:S(2)}, u32[]{:S(2)}) collective-permute-start(bf16[272,512]{1,0:T(8,128)(2,1)S(1)} %collective-permute-done.5.refs_6_), channel_id=1, source_target_pairs={{4,0},{0,4},{12,8},{8,12},{20,16},{16,20},{28,24},{24,28},{36,32},... | collective-permute-start | bytes 835592 | tf_op jit(solution)/shard_map/ppermute | solution.py:54
  20.3 0.9 %collective-permute-done.1.refs_2_ = bf16[272,512]{1,0:T(8,128)(2,1)S(1)} collective-permute-done((bf16[272,512]{1,0:T(8,128)(2,1)S(1)}, bf16[272,512]{1,0:T(8,128)(2,1)S(1)}, u32[]{:S(2)}, u32[]{:S(2)}) %collective-permute-start.1) | collective-permute-done | bytes 278560 | tf_op jit(solution)/shard_map/ppermute | solution.py:54
  21.2 1.6 %collective-permute-start.16 = (bf16[272,512]{1,0:T(8,128)(2,1)S(1)}, bf16[272,512]{1,0:T(8,128)(2,1)S(1)}, u32[]{:S(2)}, u32[]{:S(2)}) collective-permute-start(bf16[272,512]{1,0:T(8,128)(2,1)S(1)} %collective-permute-done.3.refs_4_), channel_id=1, source_target_pairs={{4,0},{0,4},{12,8},{8,12},{20,16},{16,20},{28,24},{24,28},{36,32},... | collective-permute-start | bytes 835592 | tf_op jit(solution)/shard_map/ppermute | solution.py:54
  22.9 1.8 %collective-permute-start.9 = (bf16[384,512]{1,0:T(8,128)(2,1)S(1)}, bf16[384,512]{1,0:T(8,128)(2,1)S(1)}, u32[]{:S(2)}, u32[]{:S(2)}) collective-permute-start(bf16[384,512]{1,0:T(8,128)(2,1)S(1)} %pad_maximum_fusion), channel_id=1, source_target_pairs={{16,0},{20,4},{24,8},{28,12},{0,16},{4,20},{8,24},{12,28},{48,32},... | collective-permute-start | bytes 1179656 | tf_op jit(solution)/shard_map/ppermute | solution.py:54
  24.8 1.8 %collective-permute-start.8 = (bf16[384,512]{1,0:T(8,128)(2,1)S(1)}, bf16[384,512]{1,0:T(8,128)(2,1)S(1)}, u32[]{:S(2)}, u32[]{:S(2)}) collective-permute-start(bf16[384,512]{1,0:T(8,128)(2,1)S(1)} %pad_maximum_fusion), channel_id=1, source_target_pairs={{8,0},{12,4},{16,8},{20,12},{24,16},{28,20},{0,24},{4,28},{40,32},... | collective-permute-start | bytes 1179656 | tf_op jit(solution)/shard_map/ppermute | solution.py:54
  26.6 0.6 collective-permute-start.15
  27.8 0.6 collective-permute-done.15.refs_16_
  28.4 1.5 %collective-permute-start.11 = (bf16[432,512]{1,0:T(8,128)(2,1)S(1)}, bf16[432,512]{1,0:T(8,128)(2,1)S(1)}, u32[]{:S(2)}, u32[]{:S(2)}) collective-permute-start(bf16[432,512]{1,0:T(8,128)(2,1)S(1)} %join.1), channel_id=1, source_target_pairs={{64,0},{68,4},{72,8},{76,12},{80,16},{84,20},{88,24},{92,28},{96,3... | collective-permute-start | bytes 1327112 | tf_op jit(solution)/shard_map/ppermute | solution.py:54
  29.9 1.3 %collective-permute-start.10 = (bf16[432,512]{1,0:T(8,128)(2,1)S(1)}, bf16[432,512]{1,0:T(8,128)(2,1)S(1)}, u32[]{:S(2)}, u32[]{:S(2)}) collective-permute-start(bf16[432,512]{1,0:T(8,128)(2,1)S(1)} %join.1), channel_id=1, source_target_pairs={{32,0},{36,4},{40,8},{44,12},{48,16},{52,20},{56,24},{60,28},{64,3... | collective-permute-start | bytes 1327112 | tf_op jit(solution)/shard_map/ppermute | solution.py:54
  31.4 3.8 %collective-permute-done.9.refs_10_ = bf16[384,512]{1,0:T(8,128)(2,1)S(1)} collective-permute-done((bf16[384,512]{1,0:T(8,128)(2,1)S(1)}, bf16[384,512]{1,0:T(8,128)(2,1)S(1)}, u32[]{:S(2)}, u32[]{:S(2)}) %collective-permute-start.9) | collective-permute-done | bytes 393248 | tf_op jit(solution)/shard_map/ppermute | solution.py:54
  35.2 1.1 %collective-permute-start.7 = (bf16[384,512]{1,0:T(8,128)(2,1)S(1)}, bf16[384,512]{1,0:T(8,128)(2,1)S(1)}, u32[]{:S(2)}, u32[]{:S(2)}) collective-permute-start(bf16[384,512]{1,0:T(8,128)(2,1)S(1)} %pad_maximum_fusion), channel_id=1, source_target_pairs={{24,0},{28,4},{0,8},{4,12},{8,16},{12,20},{16,24},{20,28},{56,32},... | collective-permute-start | bytes 1179656 | tf_op jit(solution)/shard_map/ppermute | solution.py:54
  36.4 7.3 %collective-permute-done.8.refs_9_ = bf16[384,512]{1,0:T(8,128)(2,1)S(1)} collective-permute-done((bf16[384,512]{1,0:T(8,128)(2,1)S(1)}, bf16[384,512]{1,0:T(8,128)(2,1)S(1)}, u32[]{:S(2)}, u32[]{:S(2)}) %collective-permute-start.8) | collective-permute-done | bytes 393248 | tf_op jit(solution)/shard_map/ppermute | solution.py:54
  43.7 0.8 collective-permute-start.22
  44.5 5.3 %collective-permute-done.10.refs_11_ = bf16[432,512]{1,0:T(8,128)(2,1)S(1)} collective-permute-done((bf16[432,512]{1,0:T(8,128)(2,1)S(1)}, bf16[432,512]{1,0:T(8,128)(2,1)S(1)}, u32[]{:S(2)}, u32[]{:S(2)}) %collective-permute-start.10) | collective-permute-done | bytes 442400 | tf_op jit(solution)/shard_map/ppermute | solution.py:54
  49.8 1.2 %collective-permute-start.23 = (bf16[432,512]{1,0:T(8,128)(2,1)S(1)}, bf16[432,512]{1,0:T(8,128)(2,1)S(1)}, u32[]{:S(2)}, u32[]{:S(2)}) collective-permute-start(bf16[432,512]{1,0:T(8,128)(2,1)S(1)} %collective-permute-done.10.refs_11_), channel_id=1, source_target_pairs={{4,0},{0,4},{12,8},{8,12},{20,16},{16,20},{28,24},{24,28},{36,32},... | collective-permute-start | bytes 1327112 | tf_op jit(solution)/shard_map/ppermute | solution.py:54
  52.5 1.5 %collective-permute-done.21.refs_22_ = bf16[384,512]{1,0:T(8,128)(2,1)S(1)} collective-permute-done((bf16[384,512]{1,0:T(8,128)(2,1)S(1)}, bf16[384,512]{1,0:T(8,128)(2,1)S(1)}, u32[]{:S(2)}, u32[]{:S(2)}) %collective-permute-start.21) | collective-permute-done | bytes 393248 | tf_op jit(solution)/shard_map/ppermute | solution.py:54
  54.6 9.1 %head.1 = (f32[256,768]{1,0:T(8,128)S(1)}, bf16[256,768]{1,0:T(8,128)(2,1)}, f32[32,2,128]{2,1,0:T(2,128)S(1)}) custom-call(bf16[272,512]{1,0:T(8,128)(2,1)S(1)} %fusion.1.refs_0_, bf16[272,512]{1,0:T(8,128)(2,1)S(1)} %collective-permute-done.refs_1_, bf16[272,512]{1,0:T(8,128)(2,1)S(1)} %collective-permute-done.1.refs_2_, ...), custom_call_target="tpu_custom_call" | custom-call | tf_op jit(solution)/shard_map/head/pallas_call | solution.py:182
  63.7 12.1 %all_to_all.10.tops_ref = f32[32,2,128]{2,1,0:T(2,128)S(1)} all-to-all(f32[32,2,128]{2,1,0:T(2,128)S(1)} %get-tuple-element.8), channel_id=1, replica_groups=mesh['pipe'=4,'tensor'=8,'dp'=4] {'pipe','tensor'}, dimensions={0} | all-to-all | bytes 65536 | tf_op jit(solution)/shard_map/all_to_all | solution.py:58
  76.3 10.7 %all_to_all.11.masses_ref = f32[32,2,128]{2,1,0:T(2,128)S(1)} all-to-all(f32[32,2,128]{2,1,0:T(2,128)S(1)} %get-tuple-element.10), channel_id=1, replica_groups=mesh['pipe'=4,'tensor'=8,'dp'=4] {'pipe','tensor'}, dimensions={0} | all-to-all | bytes 65536 | tf_op jit(solution)/shard_map/all_to_all | solution.py:58
  87.1 1.1 %share.1 = f32[256,768]{1,0:T(8,128)} custom-call(f32[32,2,128]{2,1,0:T(2,128)S(1)} %all_to_all.11.masses_ref, f32[256,768]{1,0:T(8,128)S(1)} %get-tuple-element.11.kept_ref), custom_call_target="tpu_custom_call" | custom-call | tf_op jit(solution)/shard_map/share/pallas_call | solution.py:227
  (46 shorter events, 3.7 us)
Async XLA Ops:
  2.3 9.9 %collective-permute-start.5 = (bf16[272,512]{1,0:T(8,128)(2,1)S(1)}, bf16[272,512]{1,0:T(8,128)(2,1)S(1)}, u32[]{:S(2)}, u32[]{:S(2)}) collective-permute-start(bf16[272,512]{1,0:T(8,128)(2,1)S(1)} %fusion.1.refs_0_), channel_id=1, source_target_pairs={{64,0},{68,4},{72,8},{76,12},{80,16},{84,20},{88,24},{92,28},{96,3... | collective-permute-start | bytes 835592 | tf_op jit(solution)/shard_map/ppermute | solution.py:54
  6.1 8.7 %collective-permute-start.4 = (bf16[272,512]{1,0:T(8,128)(2,1)S(1)}, bf16[272,512]{1,0:T(8,128)(2,1)S(1)}, u32[]{:S(2)}, u32[]{:S(2)}) collective-permute-start(bf16[272,512]{1,0:T(8,128)(2,1)S(1)} %fusion.1.refs_0_), channel_id=1, source_target_pairs={{16,0},{20,4},{24,8},{28,12},{0,16},{4,20},{8,24},{12,28},{48,32},... | collective-permute-start | bytes 835592 | tf_op jit(solution)/shard_map/ppermute | solution.py:54
  8.9 9.7 %collective-permute-start.3 = (bf16[272,512]{1,0:T(8,128)(2,1)S(1)}, bf16[272,512]{1,0:T(8,128)(2,1)S(1)}, u32[]{:S(2)}, u32[]{:S(2)}) collective-permute-start(bf16[272,512]{1,0:T(8,128)(2,1)S(1)} %fusion.1.refs_0_), channel_id=1, source_target_pairs={{32,0},{36,4},{40,8},{44,12},{48,16},{52,20},{56,24},{60,28},{64,3... | collective-permute-start | bytes 835592 | tf_op jit(solution)/shard_map/ppermute | solution.py:54
  9.6 10.5 %collective-permute-start.2 = (bf16[272,512]{1,0:T(8,128)(2,1)S(1)}, bf16[272,512]{1,0:T(8,128)(2,1)S(1)}, u32[]{:S(2)}, u32[]{:S(2)}) collective-permute-start(bf16[272,512]{1,0:T(8,128)(2,1)S(1)} %fusion.1.refs_0_), channel_id=1, source_target_pairs={{96,0},{100,4},{104,8},{108,12},{112,16},{116,20},{120,24},{124,28... | collective-permute-start | bytes 835592 | tf_op jit(solution)/shard_map/ppermute | solution.py:54
  10.3 10.9 %collective-permute-start.1 = (bf16[272,512]{1,0:T(8,128)(2,1)S(1)}, bf16[272,512]{1,0:T(8,128)(2,1)S(1)}, u32[]{:S(2)}, u32[]{:S(2)}) collective-permute-start(bf16[272,512]{1,0:T(8,128)(2,1)S(1)} %fusion.1.refs_0_), channel_id=1, source_target_pairs={{8,0},{12,4},{16,8},{20,12},{24,16},{28,20},{0,24},{4,28},{40,32},... | collective-permute-start | bytes 835592 | tf_op jit(solution)/shard_map/ppermute | solution.py:54
  12.2 10.7 %collective-permute-start = (bf16[272,512]{1,0:T(8,128)(2,1)S(1)}, bf16[272,512]{1,0:T(8,128)(2,1)S(1)}, u32[]{:S(2)}, u32[]{:S(2)}) collective-permute-start(bf16[272,512]{1,0:T(8,128)(2,1)S(1)} %fusion.1.refs_0_), channel_id=1, source_target_pairs={{24,0},{28,4},{0,8},{4,12},{8,16},{12,20},{16,24},{20,28},{56,32},... | collective-permute-start | bytes 835592 | tf_op jit(solution)/shard_map/ppermute | solution.py:54
  14.8 10.0 %collective-permute-start.12 = (bf16[272,512]{1,0:T(8,128)(2,1)S(1)}, bf16[272,512]{1,0:T(8,128)(2,1)S(1)}, u32[]{:S(2)}, u32[]{:S(2)}) collective-permute-start(bf16[272,512]{1,0:T(8,128)(2,1)S(1)} %fusion.1.refs_0_), channel_id=1, source_target_pairs={{4,0},{0,4},{12,8},{8,12},{20,16},{16,20},{28,24},{24,28},{36,32},... | collective-permute-start | bytes 835592 | tf_op jit(solution)/shard_map/ppermute | solution.py:54
  18.5 8.1 %collective-permute-start.18 = (bf16[272,512]{1,0:T(8,128)(2,1)S(1)}, bf16[272,512]{1,0:T(8,128)(2,1)S(1)}, u32[]{:S(2)}, u32[]{:S(2)}) collective-permute-start(bf16[272,512]{1,0:T(8,128)(2,1)S(1)} %collective-permute-done.5.refs_6_), channel_id=1, source_target_pairs={{4,0},{0,4},{12,8},{8,12},{20,16},{16,20},{28,24},{24,28},{36,32},... | collective-permute-start | bytes 835592 | tf_op jit(solution)/shard_map/ppermute | solution.py:54
  20.1 7.1 %collective-permute-start.17 = (bf16[272,512]{1,0:T(8,128)(2,1)S(1)}, bf16[272,512]{1,0:T(8,128)(2,1)S(1)}, u32[]{:S(2)}, u32[]{:S(2)}) collective-permute-start(bf16[272,512]{1,0:T(8,128)(2,1)S(1)} %collective-permute-done.4.refs_5_), channel_id=1, source_target_pairs={{4,0},{0,4},{12,8},{8,12},{20,16},{16,20},{28,24},{24,28},{36,32},... | collective-permute-start | bytes 835592 | tf_op jit(solution)/shard_map/ppermute | solution.py:54
  21.2 6.1 %collective-permute-start.16 = (bf16[272,512]{1,0:T(8,128)(2,1)S(1)}, bf16[272,512]{1,0:T(8,128)(2,1)S(1)}, u32[]{:S(2)}, u32[]{:S(2)}) collective-permute-start(bf16[272,512]{1,0:T(8,128)(2,1)S(1)} %collective-permute-done.3.refs_4_), channel_id=1, source_target_pairs={{4,0},{0,4},{12,8},{8,12},{20,16},{16,20},{28,24},{24,28},{36,32},... | collective-permute-start | bytes 835592 | tf_op jit(solution)/shard_map/ppermute | solution.py:54
  22.9 12.3 %collective-permute-start.9 = (bf16[384,512]{1,0:T(8,128)(2,1)S(1)}, bf16[384,512]{1,0:T(8,128)(2,1)S(1)}, u32[]{:S(2)}, u32[]{:S(2)}) collective-permute-start(bf16[384,512]{1,0:T(8,128)(2,1)S(1)} %pad_maximum_fusion), channel_id=1, source_target_pairs={{16,0},{20,4},{24,8},{28,12},{0,16},{4,20},{8,24},{12,28},{48,32},... | collective-permute-start | bytes 1179656 | tf_op jit(solution)/shard_map/ppermute | solution.py:54
  24.7 29.8 %slice-start = ((s8[25165824]{0:T(1024)(128)(4,1)}), s8[4194304]{0:T(1024)(128)(4,1)S(1)}, s32[]{:S(2)}) async-start(s8[25165824]{0:T(1024)(128)(4,1)} %bitcast.3), calls=%async_computation.2 | async-start | bytes 8388608
  24.7 29.8 %slice-start.1 = ((s8[25165824]{0:T(1024)(128)(4,1)}), s8[4194304]{0:T(1024)(128)(4,1)S(1)}, s32[]{:S(2)}) async-start(s8[25165824]{0:T(1024)(128)(4,1)} %bitcast.3), calls=%async_computation.3 | async-start | bytes 8388608
  24.8 29.8 %slice-start.2 = ((s8[25165824]{0:T(1024)(128)(4,1)}), s8[4194304]{0:T(1024)(128)(4,1)S(1)}, s32[]{:S(2)}) async-start(s8[25165824]{0:T(1024)(128)(4,1)} %bitcast.3), calls=%async_computation.4 | async-start | bytes 8388608
  24.8 29.8 %slice-start.3 = ((s8[25165824]{0:T(1024)(128)(4,1)}), s8[4194304]{0:T(1024)(128)(4,1)S(1)}, s32[]{:S(2)}) async-start(s8[25165824]{0:T(1024)(128)(4,1)} %bitcast.3), calls=%async_computation.5 | async-start | bytes 8388608
  24.8 29.8 %slice-start.4 = ((s8[25165824]{0:T(1024)(128)(4,1)}), s8[4194304]{0:T(1024)(128)(4,1)S(1)}, s32[]{:S(2)}) async-start(s8[25165824]{0:T(1024)(128)(4,1)} %bitcast.3), calls=%async_computation.6 | async-start | bytes 8388608
  24.8 29.8 %slice-start.5 = ((s8[25165824]{0:T(1024)(128)(4,1)}), s8[4194304]{0:T(1024)(128)(4,1)S(1)}, s32[]{:S(2)}) async-start(s8[25165824]{0:T(1024)(128)(4,1)} %bitcast.3), calls=%async_computation.7 | async-start | bytes 8388608
  24.8 18.9 %collective-permute-start.8 = (bf16[384,512]{1,0:T(8,128)(2,1)S(1)}, bf16[384,512]{1,0:T(8,128)(2,1)S(1)}, u32[]{:S(2)}, u32[]{:S(2)}) collective-permute-start(bf16[384,512]{1,0:T(8,128)(2,1)S(1)} %pad_maximum_fusion), channel_id=1, source_target_pairs={{8,0},{12,4},{16,8},{20,12},{24,16},{28,20},{0,24},{4,28},{40,32},... | collective-permute-start | bytes 1179656 | tf_op jit(solution)/shard_map/ppermute | solution.py:54
  26.6 1.8 %collective-permute-start.15 = (bf16[272,512]{1,0:T(8,128)(2,1)S(1)}, bf16[272,512]{1,0:T(8,128)(2,1)S(1)}, u32[]{:S(2)}, u32[]{:S(2)}) collective-permute-start(bf16[272,512]{1,0:T(8,128)(2,1)S(1)} %collective-permute-done.2.refs_3_), channel_id=1, source_target_pairs={{4,0},{0,4},{12,8},{8,12},{20,16},{16,20},{28,24},{24,28},{36,32},... | collective-permute-start | bytes 835592 | tf_op jit(solution)/shard_map/ppermute | solution.py:54
  27.2 2.7 %collective-permute-start.14 = (bf16[272,512]{1,0:T(8,128)(2,1)S(1)}, bf16[272,512]{1,0:T(8,128)(2,1)S(1)}, u32[]{:S(2)}, u32[]{:S(2)}) collective-permute-start(bf16[272,512]{1,0:T(8,128)(2,1)S(1)} %collective-permute-done.1.refs_2_), channel_id=1, source_target_pairs={{4,0},{0,4},{12,8},{8,12},{20,16},{16,20},{28,24},{24,28},{36,32},... | collective-permute-start | bytes 835592 | tf_op jit(solution)/shard_map/ppermute | solution.py:54
  27.3 3.9 %collective-permute-start.13 = (bf16[272,512]{1,0:T(8,128)(2,1)S(1)}, bf16[272,512]{1,0:T(8,128)(2,1)S(1)}, u32[]{:S(2)}, u32[]{:S(2)}) collective-permute-start(bf16[272,512]{1,0:T(8,128)(2,1)S(1)} %collective-permute-done.refs_1_), channel_id=1, source_target_pairs={{4,0},{0,4},{12,8},{8,12},{20,16},{16,20},{28,24},{24,28},{36,32},... | collective-permute-start | bytes 835592 | tf_op jit(solution)/shard_map/ppermute | solution.py:54
  28.4 16.1 %collective-permute-start.11 = (bf16[432,512]{1,0:T(8,128)(2,1)S(1)}, bf16[432,512]{1,0:T(8,128)(2,1)S(1)}, u32[]{:S(2)}, u32[]{:S(2)}) collective-permute-start(bf16[432,512]{1,0:T(8,128)(2,1)S(1)} %join.1), channel_id=1, source_target_pairs={{64,0},{68,4},{72,8},{76,12},{80,16},{84,20},{88,24},{92,28},{96,3... | collective-permute-start | bytes 1327112 | tf_op jit(solution)/shard_map/ppermute | solution.py:54
  29.9 19.8 %collective-permute-start.10 = (bf16[432,512]{1,0:T(8,128)(2,1)S(1)}, bf16[432,512]{1,0:T(8,128)(2,1)S(1)}, u32[]{:S(2)}, u32[]{:S(2)}) collective-permute-start(bf16[432,512]{1,0:T(8,128)(2,1)S(1)} %join.1), channel_id=1, source_target_pairs={{32,0},{36,4},{40,8},{44,12},{48,16},{52,20},{56,24},{60,28},{64,3... | collective-permute-start | bytes 1327112 | tf_op jit(solution)/shard_map/ppermute | solution.py:54
  31.2 20.3 %collective-permute-start.6 = (bf16[432,512]{1,0:T(8,128)(2,1)S(1)}, bf16[432,512]{1,0:T(8,128)(2,1)S(1)}, u32[]{:S(2)}, u32[]{:S(2)}) collective-permute-start(bf16[432,512]{1,0:T(8,128)(2,1)S(1)} %join.1), channel_id=1, source_target_pairs={{96,0},{100,4},{104,8},{108,12},{112,16},{116,20},{120,24},{124,28... | collective-permute-start | bytes 1327112 | tf_op jit(solution)/shard_map/ppermute | solution.py:54
  35.2 16.7 %collective-permute-start.7 = (bf16[384,512]{1,0:T(8,128)(2,1)S(1)}, bf16[384,512]{1,0:T(8,128)(2,1)S(1)}, u32[]{:S(2)}, u32[]{:S(2)}) collective-permute-start(bf16[384,512]{1,0:T(8,128)(2,1)S(1)} %pad_maximum_fusion), channel_id=1, source_target_pairs={{24,0},{28,4},{0,8},{4,12},{8,16},{12,20},{16,24},{20,28},{56,32},... | collective-permute-start | bytes 1179656 | tf_op jit(solution)/shard_map/ppermute | solution.py:54
  43.7 8.3 %collective-permute-start.22 = (bf16[384,512]{1,0:T(8,128)(2,1)S(1)}, bf16[384,512]{1,0:T(8,128)(2,1)S(1)}, u32[]{:S(2)}, u32[]{:S(2)}) collective-permute-start(bf16[384,512]{1,0:T(8,128)(2,1)S(1)} %collective-permute-done.9.refs_10_), channel_id=1, source_target_pairs={{4,0},{0,4},{12,8},{8,12},{20,16},{16,20},{28,24},{24,28},{36,32},... | collective-permute-start | bytes 1179656 | tf_op jit(solution)/shard_map/ppermute | solution.py:54
  44.5 10.0 %collective-permute-start.24 = (bf16[432,512]{1,0:T(8,128)(2,1)S(1)}, bf16[432,512]{1,0:T(8,128)(2,1)S(1)}, u32[]{:S(2)}, u32[]{:S(2)}) collective-permute-start(bf16[432,512]{1,0:T(8,128)(2,1)S(1)} %collective-permute-done.11.refs_12_), channel_id=1, source_target_pairs={{4,0},{0,4},{12,8},{8,12},{20,16},{16,20},{28,24},{24,28},{36,32},... | collective-permute-start | bytes 1327112 | tf_op jit(solution)/shard_map/ppermute | solution.py:54
  49.8 4.7 %collective-permute-start.23 = (bf16[432,512]{1,0:T(8,128)(2,1)S(1)}, bf16[432,512]{1,0:T(8,128)(2,1)S(1)}, u32[]{:S(2)}, u32[]{:S(2)}) collective-permute-start(bf16[432,512]{1,0:T(8,128)(2,1)S(1)} %collective-permute-done.10.refs_11_), channel_id=1, source_target_pairs={{4,0},{0,4},{12,8},{8,12},{20,16},{16,20},{28,24},{24,28},{36,32},... | collective-permute-start | bytes 1327112 | tf_op jit(solution)/shard_map/ppermute | solution.py:54
  51.5 3.0 %collective-permute-start.19 = (bf16[432,512]{1,0:T(8,128)(2,1)S(1)}, bf16[432,512]{1,0:T(8,128)(2,1)S(1)}, u32[]{:S(2)}, u32[]{:S(2)}) collective-permute-start(bf16[432,512]{1,0:T(8,128)(2,1)S(1)} %collective-permute-done.6.refs_7_), channel_id=1, source_target_pairs={{4,0},{0,4},{12,8},{8,12},{20,16},{16,20},{28,24},{24,28},{36,32},... | collective-permute-start | bytes 1327112 | tf_op jit(solution)/shard_map/ppermute | solution.py:54
  52.0 2.0 %collective-permute-start.21 = (bf16[384,512]{1,0:T(8,128)(2,1)S(1)}, bf16[384,512]{1,0:T(8,128)(2,1)S(1)}, u32[]{:S(2)}, u32[]{:S(2)}) collective-permute-start(bf16[384,512]{1,0:T(8,128)(2,1)S(1)} %collective-permute-done.8.refs_9_), channel_id=1, source_target_pairs={{4,0},{0,4},{12,8},{8,12},{20,16},{16,20},{28,24},{24,28},{36,32},... | collective-permute-start | bytes 1179656 | tf_op jit(solution)/shard_map/ppermute | solution.py:54
  52.0 2.5 %collective-permute-start.20 = (bf16[384,512]{1,0:T(8,128)(2,1)S(1)}, bf16[384,512]{1,0:T(8,128)(2,1)S(1)}, u32[]{:S(2)}, u32[]{:S(2)}) collective-permute-start(bf16[384,512]{1,0:T(8,128)(2,1)S(1)} %collective-permute-done.7.refs_8_), channel_id=1, source_target_pairs={{4,0},{0,4},{12,8},{8,12},{20,16},{16,20},{28,24},{24,28},{36,32},... | collective-permute-start | bytes 1179656 | tf_op jit(solution)/shard_map/ppermute | solution.py:54

commit v5 on v4

--- a/solution.py
+++ b/solution.py
@@ -90,34 +90,26 @@
     )(*pieces)
 
 
-def head_kernel(keys, *refs):
-    block_refs = dict(zip(keys, refs))
-    weight_ref, scores_ref, logits_ref, top_ref, normed_ref = refs[len(keys) :]
-    pipe, tensor = lax.axis_index("pipe"), lax.axis_index("tensor")
-    chip_x, core = tensor // CORES, lax.rem(tensor, CORES)
-    rows = scores_ref.shape[0]
-    width = weight_ref.shape[0] // PEERS
-    terms = [(chip, which) for chip in PLACES for which in range(CORES)]
-    groups = len(terms) // GROUP
-
-    def runs(term):
-        chip, which = terms[term]
-        at = 0
-        for array, start, count in PLACES[chip][1:]:
-            yield slice(at, at + count), block_refs[which, array].at[pl.ds(start, count), :]
-            at += count
-
-    def gain_of(term):
-        chip, which = terms[term]
-        array, start = PLACES[chip][0]
-        return block_refs[which, array][start : start + NOTE, :].astype(jnp.float32)[:1]
-
-    squares = []
+def runs_of(term, block_refs):
+    chip, which = term
+    at = 0
+    for array, start, count in PLACES[chip][1:]:
+        yield slice(at, at + count), block_refs[which, array].at[pl.ds(start, count), :]
+        at += count
+
+
+def early(term):
+    chip, which = term
+    return which == 0 or 0 in chip
+
+
+def add_squares(terms, block_refs):
+    halves = []
     for half in range(2):
         total = jnp.zeros((HALF, LANES), jnp.float32)
-        for term in range(len(terms)):
+        for term in terms:
             parts = []
-            for at, ref in runs(term):
+            for at, ref in runs_of(term, block_refs):
                 first, last = max(at.start, half * HALF), min(at.stop, (half + 1) * HALF)
                 if first < last:
                     parts.append(
@@ -127,18 +119,56 @@
                                     first - at.start : last - at.start, lane : lane + LANES
                                 ].astype(jnp.float32)
                             )
-                            for lane in range(0, width, LANES)
+                            for lane in range(0, ref.shape[1], LANES)
                         )
                     )
             total += parts[0] if len(parts) == 1 else jnp.concatenate(parts, axis=0)
-        squares.append(jnp.sum(total, axis=1, keepdims=True))
-    total_sq = jnp.concatenate(squares, axis=0)
+        halves.append(total)
+    return jnp.concatenate(halves, axis=0)
+
+
+def early_squares(blocks):
+    terms = [(chip, which) for chip in PLACES for which in range(CORES) if early((chip, which))]
+    keys = list(
+        dict.fromkeys((which, place[0]) for chip, which in terms for place in PLACES[chip])
+    )
+
+    def kernel(*refs):
+        refs[-1][...] = add_squares(terms, dict(zip(keys, refs)))
+
+    return pl.pallas_call(
+        kernel,
+        in_specs=[pl.BlockSpec(memory_space=pltpu.VMEM)] * len(keys),
+        out_specs=pl.BlockSpec(memory_space=pltpu.VMEM),
+        out_shape=jax.ShapeDtypeStruct((2 * HALF, LANES), jnp.float32),
+        compiler_params=pltpu.CompilerParams(vmem_limit_bytes=SMALL_VMEM),
+        name="early_squares",
+    )(*[blocks[key] for key in keys])
+
+
+def head_kernel(keys, *refs):
+    block_refs = dict(zip(keys, refs))
+    squares_ref, weight_ref, scores_ref, logits_ref, top_ref, normed_ref = refs[len(keys) :]
+    pipe, tensor = lax.axis_index("pipe"), lax.axis_index("tensor")
+    chip_x, core = tensor // CORES, lax.rem(tensor, CORES)
+    rows = scores_ref.shape[0]
+    width = weight_ref.shape[0] // PEERS
+    terms = [(chip, which) for chip in PLACES for which in range(CORES)]
+    groups = len(terms) // GROUP
+
+    def gain_of(term):
+        chip, which = terms[term]
+        array, start = PLACES[chip][0]
+        return block_refs[which, array][start : start + NOTE, :].astype(jnp.float32)[:1]
+
+    late = [term for term in terms if not early(term)]
+    total_sq = jnp.sum(squares_ref[...] + add_squares(late, block_refs), axis=1, keepdims=True)
     scale = lax.rsqrt(total_sq / (width * len(terms)) + 1e-05)
 
     def norm(group):
         for i, term in enumerate(range(group * GROUP, (group + 1) * GROUP)):
             gain = gain_of(term)
-            for at, ref in runs(term):
+            for at, ref in runs_of(terms[term], block_refs):
                 normed_ref[group % 2, at, i * width : (i + 1) * width] = (
                     ref[...].astype(jnp.float32) * scale[at] * gain
                 ).astype(jnp.bfloat16)
@@ -181,7 +211,7 @@
     in_vmem = pl.BlockSpec(memory_space=pltpu.VMEM)
     return pl.pallas_call(
         functools.partial(head_kernel, keys),
-        in_specs=[in_vmem] * (len(keys) + 1),
+        in_specs=[in_vmem] * (len(keys) + 2),
         out_specs=[in_vmem] * 3,
         out_shape=[
             jax.ShapeDtypeStruct((rows, columns), jnp.float32),
@@ -191,7 +221,7 @@
         scratch_shapes=[pltpu.VMEM((2, rows, GROUP * width), jnp.bfloat16)],
         compiler_params=pltpu.CompilerParams(vmem_limit_bytes=HEAD_VMEM),
         name="head",
-    )(*[blocks[key] for key in keys], weight)
+    )(*[blocks[key] for key in keys], early_squares(blocks), weight)
 
 
 def gate_kernel(tops_ref, scores_ref, kept_ref, mass_ref):

time: 88.4 us -> 87.2 us (0.986)
  waiting for transfers between devices: 24.5 us -> 23.3 us
    pallas_call x1, Pallas kernels: 9.13 us -> 7.89 us  [head(): pl.pallas_call(functools.partial(head_kernel, keys), in_specs=[in_vmem] *...]
    ppermute x25, waiting for transfers between devices: 24.5 us -> 23.3 us  [fetch(): return lax.ppermute(value, AXES, pairs)]
    pallas_call x0 -> x1, Pallas kernels: none -> 1.16 us  [early_squares(): pl.pallas_call(kernel, in_specs=[pl.BlockSpec(memory_space=pltpu.VMEM)] *...]
  transfers between devices with their start and end apart: 25 -> 25, of which waited for: 11 -> 11; matrix products, arithmetic and copies ran while one was open for 0% -> 0% of each run, Pallas kernels for 0% -> 1%
where the time goes in v5:
time: 87.2 us; the launch traced here: 86.9 us
  starting transfers between devices  27.5 us (32%)
  waiting for transfers between devices  23.3 us (27%)
  blocking collectives  22.8 us (26%)
  Pallas kernels  10.7 us (12%)
  other arithmetic  1 us (1%)
    ppermute x25, starting transfers between devices, fetch(): return lax.ppermute(value, AXES, pairs)  27.5 us
    ppermute x25, waiting for transfers between devices, fetch(): return lax.ppermute(value, AXES, pairs)  23.3 us
    all_to_all x2, blocking collectives, exchange(): return lax.all_to_all(values, AXES, 0, 0, tiled=True)  22.8 us
    pallas_call x1, Pallas kernels, head(): pl.pallas_call(functools.partial(head_kernel, keys), in_specs=[in_vmem] *...  7.89 us
  transfers between devices with their start and end apart: 25, of which 11 were waited for; matrix products, arithmetic and copies ran while one was open for 0% of the time, Pallas kernels for 1%

profile of v5, /device:TPU:1, one launch (start us, length us, event | category | flops | bytes accessed | tf_op | source)
XLA Modules:
  0.0 86.9 jit_solution(15076131070249407466)
XLA Ops:
  0.6 0.7 broadcast_in_dim.3
  1.3 1.0 %fusion.1.refs_0_ = bf16[272,512]{1,0:T(8,128)(2,1)S(1)} fusion(bf16[1,512]{1,0:T(2,128)(2,1)S(1)} %broadcast_in_dim.3, bf16[256,512]{1,0:T(8,128)(2,1)} %bitcast.6), kind=kLoop, calls=%fused_computation.3 | loop fusion | flops 835584 | bytes 541696 | tf_op jit(solution)/shard_map/concatenate | solution.py:275
  2.3 3.8 %collective-permute-start.5 = (bf16[272,512]{1,0:T(8,128)(2,1)S(1)}, bf16[272,512]{1,0:T(8,128)(2,1)S(1)}, u32[]{:S(2)}, u32[]{:S(2)}) collective-permute-start(bf16[272,512]{1,0:T(8,128)(2,1)S(1)} %fusion.1.refs_0_), channel_id=1, source_target_pairs={{64,0},{68,4},{72,8},{76,12},{80,16},{84,20},{88,24},{92,28},{96,3... | collective-permute-start | bytes 835592 | tf_op jit(solution)/shard_map/ppermute | solution.py:54
  6.1 2.7 %collective-permute-start.4 = (bf16[272,512]{1,0:T(8,128)(2,1)S(1)}, bf16[272,512]{1,0:T(8,128)(2,1)S(1)}, u32[]{:S(2)}, u32[]{:S(2)}) collective-permute-start(bf16[272,512]{1,0:T(8,128)(2,1)S(1)} %fusion.1.refs_0_), channel_id=1, source_target_pairs={{16,0},{20,4},{24,8},{28,12},{0,16},{4,20},{8,24},{12,28},{48,32},... | collective-permute-start | bytes 835592 | tf_op jit(solution)/shard_map/ppermute | solution.py:54
  8.9 0.8 collective-permute-start.3
  9.6 0.7 collective-permute-start.2
  10.3 0.9 collective-permute-start.1
  11.2 1.0 %collective-permute-done.5.refs_12_.refs_6_ = bf16[272,512]{1,0:T(8,128)(2,1)S(1)} collective-permute-done((bf16[272,512]{1,0:T(8,128)(2,1)S(1)}, bf16[272,512]{1,0:T(8,128)(2,1)S(1)}, u32[]{:S(2)}, u32[]{:S(2)}) %collective-permute-start.5) | collective-permute-done | bytes 278560 | tf_op jit(solution)/shard_map/ppermute | solution.py:54
  12.2 1.2 %collective-permute-start = (bf16[272,512]{1,0:T(8,128)(2,1)S(1)}, bf16[272,512]{1,0:T(8,128)(2,1)S(1)}, u32[]{:S(2)}, u32[]{:S(2)}) collective-permute-start(bf16[272,512]{1,0:T(8,128)(2,1)S(1)} %fusion.1.refs_0_), channel_id=1, source_target_pairs={{24,0},{28,4},{0,8},{4,12},{8,16},{12,20},{16,24},{20,28},{56,32},... | collective-permute-start | bytes 835592 | tf_op jit(solution)/shard_map/ppermute | solution.py:54
  13.4 1.4 %collective-permute-done.4.refs_10_.refs_5_ = bf16[272,512]{1,0:T(8,128)(2,1)S(1)} collective-permute-done((bf16[272,512]{1,0:T(8,128)(2,1)S(1)}, bf16[272,512]{1,0:T(8,128)(2,1)S(1)}, u32[]{:S(2)}, u32[]{:S(2)}) %collective-permute-start.4) | collective-permute-done | bytes 278560 | tf_op jit(solution)/shard_map/ppermute | solution.py:54
  14.8 2.2 %collective-permute-start.12 = (bf16[272,512]{1,0:T(8,128)(2,1)S(1)}, bf16[272,512]{1,0:T(8,128)(2,1)S(1)}, u32[]{:S(2)}, u32[]{:S(2)}) collective-permute-start(bf16[272,512]{1,0:T(8,128)(2,1)S(1)} %fusion.1.refs_0_), channel_id=1, source_target_pairs={{4,0},{0,4},{12,8},{8,12},{20,16},{16,20},{28,24},{24,28},{36,32},... | collective-permute-start | bytes 835592 | tf_op jit(solution)/shard_map/ppermute | solution.py:54
  17.0 1.5 %collective-permute-done.3.refs_8_.refs_4_ = bf16[272,512]{1,0:T(8,128)(2,1)S(1)} collective-permute-done((bf16[272,512]{1,0:T(8,128)(2,1)S(1)}, bf16[272,512]{1,0:T(8,128)(2,1)S(1)}, u32[]{:S(2)}, u32[]{:S(2)}) %collective-permute-start.3) | collective-permute-done | bytes 278560 | tf_op jit(solution)/shard_map/ppermute | solution.py:54
  18.5 1.5 %collective-permute-start.18 = (bf16[272,512]{1,0:T(8,128)(2,1)S(1)}, bf16[272,512]{1,0:T(8,128)(2,1)S(1)}, u32[]{:S(2)}, u32[]{:S(2)}) collective-permute-start(bf16[272,512]{1,0:T(8,128)(2,1)S(1)} %collective-permute-done.5.refs_12_.refs_6_), channel_id=1, source_target_pairs={{4,0},{0,4},{12,8},{8,12},{20,16},{16,20},{28,24},{24,28},{36,32},... | collective-permute-start | bytes 835592 | tf_op jit(solution)/shard_map/ppermute | solution.py:54
  20.3 0.9 %collective-permute-done.1.refs_4_.refs_2_ = bf16[272,512]{1,0:T(8,128)(2,1)S(1)} collective-permute-done((bf16[272,512]{1,0:T(8,128)(2,1)S(1)}, bf16[272,512]{1,0:T(8,128)(2,1)S(1)}, u32[]{:S(2)}, u32[]{:S(2)}) %collective-permute-start.1) | collective-permute-done | bytes 278560 | tf_op jit(solution)/shard_map/ppermute | solution.py:54
  21.2 1.6 %collective-permute-start.16 = (bf16[272,512]{1,0:T(8,128)(2,1)S(1)}, bf16[272,512]{1,0:T(8,128)(2,1)S(1)}, u32[]{:S(2)}, u32[]{:S(2)}) collective-permute-start(bf16[272,512]{1,0:T(8,128)(2,1)S(1)} %collective-permute-done.3.refs_8_.refs_4_), channel_id=1, source_target_pairs={{4,0},{0,4},{12,8},{8,12},{20,16},{16,20},{28,24},{24,28},{36,32},... | collective-permute-start | bytes 835592 | tf_op jit(solution)/shard_map/ppermute | solution.py:54
  22.9 1.8 %collective-permute-start.9 = (bf16[384,512]{1,0:T(8,128)(2,1)S(1)}, bf16[384,512]{1,0:T(8,128)(2,1)S(1)}, u32[]{:S(2)}, u32[]{:S(2)}) collective-permute-start(bf16[384,512]{1,0:T(8,128)(2,1)S(1)} %pad_maximum_fusion), channel_id=1, source_target_pairs={{16,0},{20,4},{24,8},{28,12},{0,16},{4,20},{8,24},{12,28},{48,32},... | collective-permute-start | bytes 1179656 | tf_op jit(solution)/shard_map/ppermute | solution.py:54
  24.8 1.8 %collective-permute-start.8 = (bf16[384,512]{1,0:T(8,128)(2,1)S(1)}, bf16[384,512]{1,0:T(8,128)(2,1)S(1)}, u32[]{:S(2)}, u32[]{:S(2)}) collective-permute-start(bf16[384,512]{1,0:T(8,128)(2,1)S(1)} %pad_maximum_fusion), channel_id=1, source_target_pairs={{8,0},{12,4},{16,8},{20,12},{24,16},{28,20},{0,24},{4,28},{40,32},... | collective-permute-start | bytes 1179656 | tf_op jit(solution)/shard_map/ppermute | solution.py:54
  26.6 0.6 collective-permute-start.15
  27.8 0.6 collective-permute-done.15.refs_7_.refs_16_
  28.4 1.5 %collective-permute-start.11 = (bf16[432,512]{1,0:T(8,128)(2,1)S(1)}, bf16[432,512]{1,0:T(8,128)(2,1)S(1)}, u32[]{:S(2)}, u32[]{:S(2)}) collective-permute-start(bf16[432,512]{1,0:T(8,128)(2,1)S(1)} %join.1), channel_id=1, source_target_pairs={{64,0},{68,4},{72,8},{76,12},{80,16},{84,20},{88,24},{92,28},{96,3... | collective-permute-start | bytes 1327112 | tf_op jit(solution)/shard_map/ppermute | solution.py:54
  29.9 1.3 %collective-permute-start.10 = (bf16[432,512]{1,0:T(8,128)(2,1)S(1)}, bf16[432,512]{1,0:T(8,128)(2,1)S(1)}, u32[]{:S(2)}, u32[]{:S(2)}) collective-permute-start(bf16[432,512]{1,0:T(8,128)(2,1)S(1)} %join.1), channel_id=1, source_target_pairs={{32,0},{36,4},{40,8},{44,12},{48,16},{52,20},{56,24},{60,28},{64,3... | collective-permute-start | bytes 1327112 | tf_op jit(solution)/shard_map/ppermute | solution.py:54
  31.4 3.8 %collective-permute-done.9.refs_17_.refs_10_ = bf16[384,512]{1,0:T(8,128)(2,1)S(1)} collective-permute-done((bf16[384,512]{1,0:T(8,128)(2,1)S(1)}, bf16[384,512]{1,0:T(8,128)(2,1)S(1)}, u32[]{:S(2)}, u32[]{:S(2)}) %collective-permute-start.9) | collective-permute-done | bytes 393248 | tf_op jit(solution)/shard_map/ppermute | solution.py:54
  35.2 1.1 %collective-permute-start.7 = (bf16[384,512]{1,0:T(8,128)(2,1)S(1)}, bf16[384,512]{1,0:T(8,128)(2,1)S(1)}, u32[]{:S(2)}, u32[]{:S(2)}) collective-permute-start(bf16[384,512]{1,0:T(8,128)(2,1)S(1)} %pad_maximum_fusion), channel_id=1, source_target_pairs={{24,0},{28,4},{0,8},{4,12},{8,16},{12,20},{16,24},{20,28},{56,32},... | collective-permute-start | bytes 1179656 | tf_op jit(solution)/shard_map/ppermute | solution.py:54
  36.4 7.3 %collective-permute-done.8.refs_16_.refs_9_ = bf16[384,512]{1,0:T(8,128)(2,1)S(1)} collective-permute-done((bf16[384,512]{1,0:T(8,128)(2,1)S(1)}, bf16[384,512]{1,0:T(8,128)(2,1)S(1)}, u32[]{:S(2)}, u32[]{:S(2)}) %collective-permute-start.8) | collective-permute-done | bytes 393248 | tf_op jit(solution)/shard_map/ppermute | solution.py:54
  43.7 0.8 collective-permute-start.22
  44.5 5.3 %collective-permute-done.10.refs_18_.refs_11_ = bf16[432,512]{1,0:T(8,128)(2,1)S(1)} collective-permute-done((bf16[432,512]{1,0:T(8,128)(2,1)S(1)}, bf16[432,512]{1,0:T(8,128)(2,1)S(1)}, u32[]{:S(2)}, u32[]{:S(2)}) %collective-permute-start.10) | collective-permute-done | bytes 442400 | tf_op jit(solution)/shard_map/ppermute | solution.py:54
  49.8 1.2 %collective-permute-start.23 = (bf16[432,512]{1,0:T(8,128)(2,1)S(1)}, bf16[432,512]{1,0:T(8,128)(2,1)S(1)}, u32[]{:S(2)}, u32[]{:S(2)}) collective-permute-start(bf16[432,512]{1,0:T(8,128)(2,1)S(1)} %collective-permute-done.10.refs_18_.refs_11_), channel_id=1, source_target_pairs={{4,0},{0,4},{12,8},{8,12},{20,16},{16,20},{28,24},{24,28},{36,32},... | collective-permute-start | bytes 1327112 | tf_op jit(solution)/shard_map/ppermute | solution.py:54
  52.5 1.2 %early_squares.1.refs_26_ = f32[256,128]{1,0:T(8,128)S(1)} custom-call(bf16[272,512]{1,0:T(8,128)(2,1)S(1)} %fusion.1.refs_0_, bf16[272,512]{1,0:T(8,128)(2,1)S(1)} %collective-permute-done.12.refs_1_.refs_13_, bf16[272,512]{1,0:T(8,128)(2,1)S(1)} %collective-permute-done.refs_2_.refs_1_, bf16[272,512]{1,0:T(8,128)(2,1)S(1)} %collective-permute-done.13.refs_3_.refs_14_, ...), custom_call_target="tpu_custom_call" | custom-call | tf_op jit(solution)/shard_map/early_squares/pallas_call | solution.py:139
  54.6 7.9 %head.1 = (f32[256,768]{1,0:T(8,128)S(1)}, bf16[256,768]{1,0:T(8,128)(2,1)}, f32[32,2,128]{2,1,0:T(2,128)S(1)}) custom-call(bf16[272,512]{1,0:T(8,128)(2,1)S(1)} %fusion.1.refs_0_, bf16[272,512]{1,0:T(8,128)(2,1)S(1)} %collective-permute-done.refs_2_.refs_1_, bf16[272,512]{1,0:T(8,128)(2,1)S(1)} %collective-permute-done.1.refs_4_.refs_2_, ...), custom_call_target="tpu_custom_call" | custom-call | tf_op jit(solution)/shard_map/head/pallas_call | solution.py:212
  62.5 12.1 %all_to_all.10.tops_ref = f32[32,2,128]{2,1,0:T(2,128)S(1)} all-to-all(f32[32,2,128]{2,1,0:T(2,128)S(1)} %get-tuple-element.8), channel_id=1, replica_groups=mesh['pipe'=4,'tensor'=8,'dp'=4] {'pipe','tensor'}, dimensions={0} | all-to-all | bytes 65536 | tf_op jit(solution)/shard_map/all_to_all | solution.py:58
  75.1 10.7 %all_to_all.11.masses_ref = f32[32,2,128]{2,1,0:T(2,128)S(1)} all-to-all(f32[32,2,128]{2,1,0:T(2,128)S(1)} %get-tuple-element.10), channel_id=1, replica_groups=mesh['pipe'=4,'tensor'=8,'dp'=4] {'pipe','tensor'}, dimensions={0} | all-to-all | bytes 65536 | tf_op jit(solution)/shard_map/all_to_all | solution.py:58
  85.8 1.1 %share.1 = f32[256,768]{1,0:T(8,128)} custom-call(f32[32,2,128]{2,1,0:T(2,128)S(1)} %all_to_all.11.masses_ref, f32[256,768]{1,0:T(8,128)S(1)} %get-tuple-element.11.kept_ref), custom_call_target="tpu_custom_call" | custom-call | tf_op jit(solution)/shard_map/share/pallas_call | solution.py:257
  (47 shorter events, 4.0 us)
Async XLA Ops:
  2.3 9.9 %collective-permute-start.5 = (bf16[272,512]{1,0:T(8,128)(2,1)S(1)}, bf16[272,512]{1,0:T(8,128)(2,1)S(1)}, u32[]{:S(2)}, u32[]{:S(2)}) collective-permute-start(bf16[272,512]{1,0:T(8,128)(2,1)S(1)} %fusion.1.refs_0_), channel_id=1, source_target_pairs={{64,0},{68,4},{72,8},{76,12},{80,16},{84,20},{88,24},{92,28},{96,3... | collective-permute-start | bytes 835592 | tf_op jit(solution)/shard_map/ppermute | solution.py:54
  6.1 8.7 %collective-permute-start.4 = (bf16[272,512]{1,0:T(8,128)(2,1)S(1)}, bf16[272,512]{1,0:T(8,128)(2,1)S(1)}, u32[]{:S(2)}, u32[]{:S(2)}) collective-permute-start(bf16[272,512]{1,0:T(8,128)(2,1)S(1)} %fusion.1.refs_0_), channel_id=1, source_target_pairs={{16,0},{20,4},{24,8},{28,12},{0,16},{4,20},{8,24},{12,28},{48,32},... | collective-permute-start | bytes 835592 | tf_op jit(solution)/shard_map/ppermute | solution.py:54
  8.9 9.7 %collective-permute-start.3 = (bf16[272,512]{1,0:T(8,128)(2,1)S(1)}, bf16[272,512]{1,0:T(8,128)(2,1)S(1)}, u32[]{:S(2)}, u32[]{:S(2)}) collective-permute-start(bf16[272,512]{1,0:T(8,128)(2,1)S(1)} %fusion.1.refs_0_), channel_id=1, source_target_pairs={{32,0},{36,4},{40,8},{44,12},{48,16},{52,20},{56,24},{60,28},{64,3... | collective-permute-start | bytes 835592 | tf_op jit(solution)/shard_map/ppermute | solution.py:54
  9.6 10.5 %collective-permute-start.2 = (bf16[272,512]{1,0:T(8,128)(2,1)S(1)}, bf16[272,512]{1,0:T(8,128)(2,1)S(1)}, u32[]{:S(2)}, u32[]{:S(2)}) collective-permute-start(bf16[272,512]{1,0:T(8,128)(2,1)S(1)} %fusion.1.refs_0_), channel_id=1, source_target_pairs={{96,0},{100,4},{104,8},{108,12},{112,16},{116,20},{120,24},{124,28... | collective-permute-start | bytes 835592 | tf_op jit(solution)/shard_map/ppermute | solution.py:54
  10.3 10.9 %collective-permute-start.1 = (bf16[272,512]{1,0:T(8,128)(2,1)S(1)}, bf16[272,512]{1,0:T(8,128)(2,1)S(1)}, u32[]{:S(2)}, u32[]{:S(2)}) collective-permute-start(bf16[272,512]{1,0:T(8,128)(2,1)S(1)} %fusion.1.refs_0_), channel_id=1, source_target_pairs={{8,0},{12,4},{16,8},{20,12},{24,16},{28,20},{0,24},{4,28},{40,32},... | collective-permute-start | bytes 835592 | tf_op jit(solution)/shard_map/ppermute | solution.py:54
  12.2 10.7 %collective-permute-start = (bf16[272,512]{1,0:T(8,128)(2,1)S(1)}, bf16[272,512]{1,0:T(8,128)(2,1)S(1)}, u32[]{:S(2)}, u32[]{:S(2)}) collective-permute-start(bf16[272,512]{1,0:T(8,128)(2,1)S(1)} %fusion.1.refs_0_), channel_id=1, source_target_pairs={{24,0},{28,4},{0,8},{4,12},{8,16},{12,20},{16,24},{20,28},{56,32},... | collective-permute-start | bytes 835592 | tf_op jit(solution)/shard_map/ppermute | solution.py:54
  14.8 10.0 %collective-permute-start.12 = (bf16[272,512]{1,0:T(8,128)(2,1)S(1)}, bf16[272,512]{1,0:T(8,128)(2,1)S(1)}, u32[]{:S(2)}, u32[]{:S(2)}) collective-permute-start(bf16[272,512]{1,0:T(8,128)(2,1)S(1)} %fusion.1.refs_0_), channel_id=1, source_target_pairs={{4,0},{0,4},{12,8},{8,12},{20,16},{16,20},{28,24},{24,28},{36,32},... | collective-permute-start | bytes 835592 | tf_op jit(solution)/shard_map/ppermute | solution.py:54
  18.5 8.1 %collective-permute-start.18 = (bf16[272,512]{1,0:T(8,128)(2,1)S(1)}, bf16[272,512]{1,0:T(8,128)(2,1)S(1)}, u32[]{:S(2)}, u32[]{:S(2)}) collective-permute-start(bf16[272,512]{1,0:T(8,128)(2,1)S(1)} %collective-permute-done.5.refs_12_.refs_6_), channel_id=1, source_target_pairs={{4,0},{0,4},{12,8},{8,12},{20,16},{16,20},{28,24},{24,28},{36,32},... | collective-permute-start | bytes 835592 | tf_op jit(solution)/shard_map/ppermute | solution.py:54
  20.1 7.1 %collective-permute-start.17 = (bf16[272,512]{1,0:T(8,128)(2,1)S(1)}, bf16[272,512]{1,0:T(8,128)(2,1)S(1)}, u32[]{:S(2)}, u32[]{:S(2)}) collective-permute-start(bf16[272,512]{1,0:T(8,128)(2,1)S(1)} %collective-permute-done.4.refs_10_.refs_5_), channel_id=1, source_target_pairs={{4,0},{0,4},{12,8},{8,12},{20,16},{16,20},{28,24},{24,28},{36,32},... | collective-permute-start | bytes 835592 | tf_op jit(solution)/shard_map/ppermute | solution.py:54
  21.2 6.1 %collective-permute-start.16 = (bf16[272,512]{1,0:T(8,128)(2,1)S(1)}, bf16[272,512]{1,0:T(8,128)(2,1)S(1)}, u32[]{:S(2)}, u32[]{:S(2)}) collective-permute-start(bf16[272,512]{1,0:T(8,128)(2,1)S(1)} %collective-permute-done.3.refs_8_.refs_4_), channel_id=1, source_target_pairs={{4,0},{0,4},{12,8},{8,12},{20,16},{16,20},{28,24},{24,28},{36,32},... | collective-permute-start | bytes 835592 | tf_op jit(solution)/shard_map/ppermute | solution.py:54
  22.9 12.3 %collective-permute-start.9 = (bf16[384,512]{1,0:T(8,128)(2,1)S(1)}, bf16[384,512]{1,0:T(8,128)(2,1)S(1)}, u32[]{:S(2)}, u32[]{:S(2)}) collective-permute-start(bf16[384,512]{1,0:T(8,128)(2,1)S(1)} %pad_maximum_fusion), channel_id=1, source_target_pairs={{16,0},{20,4},{24,8},{28,12},{0,16},{4,20},{8,24},{12,28},{48,32},... | collective-permute-start | bytes 1179656 | tf_op jit(solution)/shard_map/ppermute | solution.py:54
  24.7 29.8 %slice-start = ((s8[25165824]{0:T(1024)(128)(4,1)}), s8[4194304]{0:T(1024)(128)(4,1)S(1)}, s32[]{:S(2)}) async-start(s8[25165824]{0:T(1024)(128)(4,1)} %bitcast.3), calls=%async_computation.2 | async-start | bytes 8388608
  24.7 29.8 %slice-start.1 = ((s8[25165824]{0:T(1024)(128)(4,1)}), s8[4194304]{0:T(1024)(128)(4,1)S(1)}, s32[]{:S(2)}) async-start(s8[25165824]{0:T(1024)(128)(4,1)} %bitcast.3), calls=%async_computation.3 | async-start | bytes 8388608
  24.8 29.8 %slice-start.2 = ((s8[25165824]{0:T(1024)(128)(4,1)}), s8[4194304]{0:T(1024)(128)(4,1)S(1)}, s32[]{:S(2)}) async-start(s8[25165824]{0:T(1024)(128)(4,1)} %bitcast.3), calls=%async_computation.4 | async-start | bytes 8388608
  24.8 29.8 %slice-start.3 = ((s8[25165824]{0:T(1024)(128)(4,1)}), s8[4194304]{0:T(1024)(128)(4,1)S(1)}, s32[]{:S(2)}) async-start(s8[25165824]{0:T(1024)(128)(4,1)} %bitcast.3), calls=%async_computation.5 | async-start | bytes 8388608
  24.8 29.8 %slice-start.4 = ((s8[25165824]{0:T(1024)(128)(4,1)}), s8[4194304]{0:T(1024)(128)(4,1)S(1)}, s32[]{:S(2)}) async-start(s8[25165824]{0:T(1024)(128)(4,1)} %bitcast.3), calls=%async_computation.6 | async-start | bytes 8388608
  24.8 29.8 %slice-start.5 = ((s8[25165824]{0:T(1024)(128)(4,1)}), s8[4194304]{0:T(1024)(128)(4,1)S(1)}, s32[]{:S(2)}) async-start(s8[25165824]{0:T(1024)(128)(4,1)} %bitcast.3), calls=%async_computation.7 | async-start | bytes 8388608
  24.8 18.9 %collective-permute-start.8 = (bf16[384,512]{1,0:T(8,128)(2,1)S(1)}, bf16[384,512]{1,0:T(8,128)(2,1)S(1)}, u32[]{:S(2)}, u32[]{:S(2)}) collective-permute-start(bf16[384,512]{1,0:T(8,128)(2,1)S(1)} %pad_maximum_fusion), channel_id=1, source_target_pairs={{8,0},{12,4},{16,8},{20,12},{24,16},{28,20},{0,24},{4,28},{40,32},... | collective-permute-start | bytes 1179656 | tf_op jit(solution)/shard_map/ppermute | solution.py:54
  26.6 1.8 %collective-permute-start.15 = (bf16[272,512]{1,0:T(8,128)(2,1)S(1)}, bf16[272,512]{1,0:T(8,128)(2,1)S(1)}, u32[]{:S(2)}, u32[]{:S(2)}) collective-permute-start(bf16[272,512]{1,0:T(8,128)(2,1)S(1)} %collective-permute-done.2.refs_6_.refs_3_), channel_id=1, source_target_pairs={{4,0},{0,4},{12,8},{8,12},{20,16},{16,20},{28,24},{24,28},{36,32},... | collective-permute-start | bytes 835592 | tf_op jit(solution)/shard_map/ppermute | solution.py:54
  27.2 2.7 %collective-permute-start.14 = (bf16[272,512]{1,0:T(8,128)(2,1)S(1)}, bf16[272,512]{1,0:T(8,128)(2,1)S(1)}, u32[]{:S(2)}, u32[]{:S(2)}) collective-permute-start(bf16[272,512]{1,0:T(8,128)(2,1)S(1)} %collective-permute-done.1.refs_4_.refs_2_), channel_id=1, source_target_pairs={{4,0},{0,4},{12,8},{8,12},{20,16},{16,20},{28,24},{24,28},{36,32},... | collective-permute-start | bytes 835592 | tf_op jit(solution)/shard_map/ppermute | solution.py:54
  27.3 3.9 %collective-permute-start.13 = (bf16[272,512]{1,0:T(8,128)(2,1)S(1)}, bf16[272,512]{1,0:T(8,128)(2,1)S(1)}, u32[]{:S(2)}, u32[]{:S(2)}) collective-permute-start(bf16[272,512]{1,0:T(8,128)(2,1)S(1)} %collective-permute-done.refs_2_.refs_1_), channel_id=1, source_target_pairs={{4,0},{0,4},{12,8},{8,12},{20,16},{16,20},{28,24},{24,28},{36,32},... | collective-permute-start | bytes 835592 | tf_op jit(solution)/shard_map/ppermute | solution.py:54
  28.4 16.1 %collective-permute-start.11 = (bf16[432,512]{1,0:T(8,128)(2,1)S(1)}, bf16[432,512]{1,0:T(8,128)(2,1)S(1)}, u32[]{:S(2)}, u32[]{:S(2)}) collective-permute-start(bf16[432,512]{1,0:T(8,128)(2,1)S(1)} %join.1), channel_id=1, source_target_pairs={{64,0},{68,4},{72,8},{76,12},{80,16},{84,20},{88,24},{92,28},{96,3... | collective-permute-start | bytes 1327112 | tf_op jit(solution)/shard_map/ppermute | solution.py:54
  29.9 19.8 %collective-permute-start.10 = (bf16[432,512]{1,0:T(8,128)(2,1)S(1)}, bf16[432,512]{1,0:T(8,128)(2,1)S(1)}, u32[]{:S(2)}, u32[]{:S(2)}) collective-permute-start(bf16[432,512]{1,0:T(8,128)(2,1)S(1)} %join.1), channel_id=1, source_target_pairs={{32,0},{36,4},{40,8},{44,12},{48,16},{52,20},{56,24},{60,28},{64,3... | collective-permute-start | bytes 1327112 | tf_op jit(solution)/shard_map/ppermute | solution.py:54
  31.2 20.3 %collective-permute-start.6 = (bf16[432,512]{1,0:T(8,128)(2,1)S(1)}, bf16[432,512]{1,0:T(8,128)(2,1)S(1)}, u32[]{:S(2)}, u32[]{:S(2)}) collective-permute-start(bf16[432,512]{1,0:T(8,128)(2,1)S(1)} %join.1), channel_id=1, source_target_pairs={{96,0},{100,4},{104,8},{108,12},{112,16},{116,20},{120,24},{124,28... | collective-permute-start | bytes 1327112 | tf_op jit(solution)/shard_map/ppermute | solution.py:54
  35.2 16.7 %collective-permute-start.7 = (bf16[384,512]{1,0:T(8,128)(2,1)S(1)}, bf16[384,512]{1,0:T(8,128)(2,1)S(1)}, u32[]{:S(2)}, u32[]{:S(2)}) collective-permute-start(bf16[384,512]{1,0:T(8,128)(2,1)S(1)} %pad_maximum_fusion), channel_id=1, source_target_pairs={{24,0},{28,4},{0,8},{4,12},{8,16},{12,20},{16,24},{20,28},{56,32},... | collective-permute-start | bytes 1179656 | tf_op jit(solution)/shard_map/ppermute | solution.py:54
  43.7 8.3 %collective-permute-start.22 = (bf16[384,512]{1,0:T(8,128)(2,1)S(1)}, bf16[384,512]{1,0:T(8,128)(2,1)S(1)}, u32[]{:S(2)}, u32[]{:S(2)}) collective-permute-start(bf16[384,512]{1,0:T(8,128)(2,1)S(1)} %collective-permute-done.9.refs_17_.refs_10_), channel_id=1, source_target_pairs={{4,0},{0,4},{12,8},{8,12},{20,16},{16,20},{28,24},{24,28},{36,32},... | collective-permute-start | bytes 1179656 | tf_op jit(solution)/shard_map/ppermute | solution.py:54
  44.5 10.0 %collective-permute-start.24 = (bf16[432,512]{1,0:T(8,128)(2,1)S(1)}, bf16[432,512]{1,0:T(8,128)(2,1)S(1)}, u32[]{:S(2)}, u32[]{:S(2)}) collective-permute-start(bf16[432,512]{1,0:T(8,128)(2,1)S(1)} %collective-permute-done.11.refs_19_.refs_12_), channel_id=1, source_target_pairs={{4,0},{0,4},{12,8},{8,12},{20,16},{16,20},{28,24},{24,28},{36,32},... | collective-permute-start | bytes 1327112 | tf_op jit(solution)/shard_map/ppermute | solution.py:54
  49.8 4.7 %collective-permute-start.23 = (bf16[432,512]{1,0:T(8,128)(2,1)S(1)}, bf16[432,512]{1,0:T(8,128)(2,1)S(1)}, u32[]{:S(2)}, u32[]{:S(2)}) collective-permute-start(bf16[432,512]{1,0:T(8,128)(2,1)S(1)} %collective-permute-done.10.refs_18_.refs_11_), channel_id=1, source_target_pairs={{4,0},{0,4},{12,8},{8,12},{20,16},{16,20},{28,24},{24,28},{36,32},... | collective-permute-start | bytes 1327112 | tf_op jit(solution)/shard_map/ppermute | solution.py:54
  51.5 3.0 %collective-permute-start.19 = (bf16[432,512]{1,0:T(8,128)(2,1)S(1)}, bf16[432,512]{1,0:T(8,128)(2,1)S(1)}, u32[]{:S(2)}, u32[]{:S(2)}) collective-permute-start(bf16[432,512]{1,0:T(8,128)(2,1)S(1)} %collective-permute-done.6.refs_14_.refs_7_), channel_id=1, source_target_pairs={{4,0},{0,4},{12,8},{8,12},{20,16},{16,20},{28,24},{24,28},{36,32},... | collective-permute-start | bytes 1327112 | tf_op jit(solution)/shard_map/ppermute | solution.py:54
  52.0 2.0 %collective-permute-start.21 = (bf16[384,512]{1,0:T(8,128)(2,1)S(1)}, bf16[384,512]{1,0:T(8,128)(2,1)S(1)}, u32[]{:S(2)}, u32[]{:S(2)}) collective-permute-start(bf16[384,512]{1,0:T(8,128)(2,1)S(1)} %collective-permute-done.8.refs_16_.refs_9_), channel_id=1, source_target_pairs={{4,0},{0,4},{12,8},{8,12},{20,16},{16,20},{28,24},{24,28},{36,32},... | collective-permute-start | bytes 1179656 | tf_op jit(solution)/shard_map/ppermute | solution.py:54
  52.0 2.5 %collective-permute-start.20 = (bf16[384,512]{1,0:T(8,128)(2,1)S(1)}, bf16[384,512]{1,0:T(8,128)(2,1)S(1)}, u32[]{:S(2)}, u32[]{:S(2)}) collective-permute-start(bf16[384,512]{1,0:T(8,128)(2,1)S(1)} %collective-permute-done.7.refs_15_.refs_8_), channel_id=1, source_target_pairs={{4,0},{0,4},{12,8},{8,12},{20,16},{16,20},{28,24},{24,28},{36,32},... | collective-permute-start | bytes 1179656 | tf_op jit(solution)/shard_map/ppermute | solution.py:54
